TPU v7x, 32 devices: a whole 2x2x4 slice. The times are simulated.
32 devices in a mesh: row: 16 (over z, y, x), col: 2 (over core).
Axes of the slice: x: 2, y: 2, z: 4, core: 2. Of those that a mesh axis runs over, the one named last changes fastest.
Arguments:
- rhs: float32 [16, 2, 12, 192, 128], P('row', 'col'), may hold values from -6 to 6
- smoother: bfloat16 [16, 2, 3, 3, 768], P('row', 'col'), may hold values from -0.375 to 2.375
- blocks: bfloat16 [16, 2, 12, 192, 1536], P('row', 'col'), may hold values from -0.15625 to 0.15625
- col_index: int32 [16, 2, 12, 8], P('row', 'col'), may hold values from 0 to 27, as said below
- send_list: int32 [16, 2, 4, 4], P('row', 'col'), may hold values from 0 to 11, as said below
- agg_id: int32 [16, 2, 12], P('row', 'col'), may hold values from 0 to 3, as said below
- prolong: bfloat16 [16, 2, 6, 2304], P('row', 'col'), may hold values from -0.4375 to 0.4375
- coarse_inverse: bfloat16 [768, 768], P('row'), may hold values from -0.21875 to 0.21875
Outputs:
- smoothed_solution: float32 [16, 2, 12, 192, 128], P('row', 'col')
Inputs may be any that keep to these rules, and one draw needn't show every extreme that they name: `col_index`: A value below 12 names a block row of the same device; the value 12 + 4 * g + j names slot j of ghost group g. Every ghost slot is named by some entry of each device. `send_list`: the 4 blocks of one device and group are distinct. `agg_id`: every aggregate of a device holds at least one block row.
All inputs are finite; a program needn't handle non-finite values.
Results may differ from a plain program's by a relative error of at most 0.0029.
Values may be sent and summed in bfloat16 or wider, within the bound.
A program may use at most 64 MiB of HBM per device.

v0:
```python
import jax
import jax.numpy as jnp
from jax import lax
from jax.sharding import PartitionSpec as P

damping = 0.6


def passed_along(value, axis, steps):
    count = lax.axis_size(axis)
    pairs = [(source, (source + steps) % count) for source in range(count)]
    return lax.ppermute(value, axis, pairs)


def point_smooth(coefficients, vector):
    leading = vector.shape[:2]
    blocks = vector.shape[2]
    grains = vector.shape[3] // 3
    columns = vector.shape[4]
    factors = coefficients.astype(jnp.float32).reshape(leading + (3, 3, blocks, grains))
    pieces = vector.reshape(leading + (blocks, 3, grains, columns))
    outputs = []
    for component in range(3):
        summed = factors[:, :, component, 0, :, :, None] * pieces[:, :, :, 0]
        summed = summed + factors[:, :, component, 1, :, :, None] * pieces[:, :, :, 1]
        summed = summed + factors[:, :, component, 2, :, :, None] * pieces[:, :, :, 2]
        outputs.append(summed)
    return damping * jnp.stack(outputs, axis=3).reshape(vector.shape)


def body(rhs, smoother, blocks, col_index, send_list, agg_id, prolong, coarse_inverse):
    block_count = rhs.shape[2]
    dof_count = rhs.shape[3]
    vectors = rhs.shape[4]
    send_rows = send_list[0, 0]
    coarse_dofs = prolong.shape[2]
    shaped = prolong[0, 0].reshape((coarse_dofs, block_count, dof_count))

    def apply_operator(vector, ready_ghosts=None):
        vector_low = vector.astype(jnp.bfloat16)
        shard_low = vector_low[0, 0]
        ghosts = []
        for offset in (1, -1):
            packed = jnp.take(shard_low, send_rows[0 if offset == 1 else 1], axis=0)
            ghosts.append(passed_along(packed, "row", offset))
        for offset in (1, -1):
            packed = jnp.take(shard_low, send_rows[2 if offset == 1 else 3], axis=0)
            ghosts.append(passed_along(packed, "col", offset))
        source = jnp.concatenate([shard_low] + list(ghosts), axis=0)
        columns = col_index[0, 0]
        picked = jnp.take(source, columns.reshape(-1), axis=0).reshape((block_count, -1, vectors))
        product = jnp.einsum(
            "nde,ner->ndr", blocks[0, 0], picked, preferred_element_type=jnp.float32
        )
        return product[None, None]

    first_iter = point_smooth(smoother, rhs)
    residual_first = rhs - apply_operator(first_iter)
    update_second = point_smooth(smoother, residual_first)
    second_iter = first_iter + update_second
    residual_second = residual_first - apply_operator(update_second)
    coarse_rows = coarse_inverse.shape[1] // (lax.axis_size("row") * lax.axis_size("col"))
    aggregates = coarse_rows // coarse_dofs
    onehot = (agg_id[0, 0][None, :] == jnp.arange(aggregates, dtype=jnp.int32)[:, None]).astype(
        jnp.float32
    )
    local_terms = jnp.einsum(
        "knd,ndr->nkr",
        shaped,
        residual_second[0, 0].astype(jnp.bfloat16),
        preferred_element_type=jnp.float32,
    )
    coarse_residual = jnp.einsum(
        "an,nkr->akr", onehot, local_terms, precision=lax.Precision.HIGHEST
    )
    coarse_rhs = coarse_residual.astype(jnp.bfloat16).reshape((coarse_rows, vectors))
    column_place = lax.axis_index("col") * coarse_rows
    coarse_solution = jnp.dot(
        coarse_inverse,
        lax.all_gather(coarse_rhs, ("row", "col"), axis=0, tiled=True),
        preferred_element_type=jnp.float32,
    )
    coarse_solution = lax.dynamic_slice_in_dim(coarse_solution, column_place, coarse_rows, 0)
    coarse_rounded = coarse_solution.astype(jnp.bfloat16).reshape(
        (aggregates, coarse_dofs, vectors)
    )
    chosen = jnp.einsum(
        "an,akr->nkr",
        onehot.astype(jnp.bfloat16),
        coarse_rounded,
        preferred_element_type=jnp.float32,
    ).astype(jnp.bfloat16)
    correction = jnp.einsum("knd,nkr->ndr", shaped, chosen, preferred_element_type=jnp.float32)[
        None, None
    ]
    after_coarse = second_iter + correction
    residual_third = residual_second - apply_operator(correction)
    return after_coarse + point_smooth(smoother, residual_third)


def solution(mesh):
    placed = (
        P("row", "col", None, None, None),
        P("row", "col", None, None, None),
        P("row", "col", None, None, None),
        P("row", "col", None, None),
        P("row", "col", None, None),
        P("row", "col", None),
        P("row", "col", None, None),
        P("row", None),
    )
    return jax.shard_map(
        body,
        mesh=mesh,
        in_specs=placed,
        out_specs=P("row", "col", None, None, None),
        check_vma=False,
    )
```

profile of v0, /device:TPU:0, one launch (start us, length us, event | category | flops | bytes accessed | tf_op | source)
XLA Modules:
  0.0 137.2 jit_solution(16454642854752045829)
XLA Ops:
  0.0 0.8 compare_and_fusion.1
  0.9 0.8 reshape.218
  1.7 2.9 %multiply_add_fusion.8 = (f32[1,1,12,1,64,128]{5,4,3,2,1,0:T(8,128)S(1)}, f32[1,1,12,1,64,128]{5,4,3,2,1,0:T(8,128)S(1)}, f32[1,1,12,1,64,128]{5,4,3,2,1,0:T(8,128)S(1)}) fusion(f32[1,1,12,3,64,128]{5,4,3,2,1,0:T(8,128)} %bitcast.111, f32[12,64]{1,0:T(8,128)S(1)} %get-tuple-element.35, f32[12,64]{1,0:T(8,128)S(1)} %get-tuple-element.36, ...), kind=kLoop, calls=%fused_computation.50 | loop fusion | flops 1474560 | bytes 2386944 | tf_op jit(solution)/shard_map/add | solution.py:26
  4.8 0.6 gather_fusion
  5.5 3.0 %collective-permute-start = (bf16[4,192,128]{2,1,0:T(8,128)(2,1)S(1)}, bf16[4,192,128]{2,1,0:T(8,128)(2,1)S(1)}, u32[]{:S(2)}, u32[]{:S(2)}) collective-permute-start(bf16[4,192,128]{2,1,0:T(8,128)(2,1)S(1)} %broadcast_select_fusion.14), channel_id=1, source_target_pairs={{0,2},{2,4},{4,6},{6,8},{8,10},{10,12},{12,14},{14,16},{16,18},{18... | collective-permute-start | bytes 589832 | tf_op jit(solution)/shard_map/ppermute | solution.py:12
  8.5 0.6 gather_fusion.1
  9.2 4.1 %collective-permute-start.1 = (bf16[4,192,128]{2,1,0:T(8,128)(2,1)S(1)}, bf16[4,192,128]{2,1,0:T(8,128)(2,1)S(1)}, u32[]{:S(2)}, u32[]{:S(2)}) collective-permute-start(bf16[4,192,128]{2,1,0:T(8,128)(2,1)S(1)} %broadcast_select_fusion.11), channel_id=1, source_target_pairs={{0,30},{2,0},{4,2},{6,4},{8,6},{10,8},{12,10},{14,12},{16,14},{18,... | collective-permute-start | bytes 589832 | tf_op jit(solution)/shard_map/ppermute | solution.py:12
  13.3 0.6 gather_fusion.2
  14.0 0.6 gather_fusion.3
  14.7 0.6 collective-permute-start.3
  15.6 0.9 constant_dynamic-update-slice_fusion.4
  16.5 1.0 collective-permute-done
  17.5 0.7 constant_dynamic-update-slice_fusion.3
  18.2 0.6 collective-permute-done.1
  18.8 0.7 constant_dynamic-update-slice_fusion.2
  19.5 0.7 constant_dynamic-update-slice_fusion.1
  20.2 0.7 constant_dynamic-update-slice_fusion
  20.9 4.9 %gather_fusion.4 = bf16[96,192,128]{2,1,0:T(8,128)(2,1)} fusion(bf16[28,192,128]{2,1,0:T(8,128)(2,1)} %constant_dynamic-update-slice_fusion, s32[1024]{0:T(1024)S(1)} %pad_clamp_fusion), kind=kCustom, calls=%fused_computation.1.clone | custom fusion | bytes 9437568 | tf_op jit(solution)/shard_map/jit(_take)/gather | solution.py:51
  25.8 3.0 %broadcast_select_fusion.2 = bf16[96,192,128]{2,1,0:T(8,128)(2,1)S(1)} fusion(bf16[96,192,128]{2,1,0:T(8,128)(2,1)} %gather_fusion.4, pred[96]{0:T(512)(128)(4,1)S(1)} %compare_and_fusion), kind=kLoop, calls=%fused_computation.23 | loop fusion | flops 2359296 | bytes 9437280 | tf_op jit(solution)/shard_map/jit(_take)/select_n | solution.py:51
  28.8 1.0 slice-done.1
  29.8 2.0 %fusion.15 = f32[1,1,12,192,128]{4,3,2,1,0:T(8,128)S(1)} fusion(f32[1,1,12,192,128]{4,3,2,1,0:T(8,128)S(1)} %copy-done.5, bf16[12,1536,128]{2,1,0:T(8,128)(2,1)S(1)} %bitcast.109, bf16[1,1,12,192,1536]{4,3,2,1,0:T(8,128)(2,1)S(1)} %bitcast.102), kind=kOutput, calls=%fused_computation.28 | convolution fusion | flops 906264576 | bytes 14155776 | tf_op jit(solution)/shard_map/nde,ner->ndr/dot_general | solution.py:52
  31.8 1.2 multiply_add_fusion.5
  33.3 1.3 fusion.25
  34.6 0.6 gather_fusion.8
  35.2 0.6 gather_fusion.7
  35.8 0.6 gather_fusion.6
  36.4 0.6 gather_fusion.5
  37.3 1.5 %collective-permute-start.4 = (bf16[4,192,128]{2,1,0:T(8,128)(2,1)S(1)}, bf16[4,192,128]{2,1,0:T(8,128)(2,1)S(1)}, u32[]{:S(2)}, u32[]{:S(2)}) collective-permute-start(bf16[4,192,128]{2,1,0:T(8,128)(2,1)S(1)} %broadcast_select_fusion.13), channel_id=1, source_target_pairs={{0,2},{2,4},{4,6},{6,8},{8,10},{10,12},{12,14},{14,16},{16,18},{18... | collective-permute-start | bytes 589832 | tf_op jit(solution)/shard_map/ppermute | solution.py:12
  38.9 4.2 %collective-permute-start.5 = (bf16[4,192,128]{2,1,0:T(8,128)(2,1)S(1)}, bf16[4,192,128]{2,1,0:T(8,128)(2,1)S(1)}, u32[]{:S(2)}, u32[]{:S(2)}) collective-permute-start(bf16[4,192,128]{2,1,0:T(8,128)(2,1)S(1)} %broadcast_select_fusion.10), channel_id=1, source_target_pairs={{0,30},{2,0},{4,2},{6,4},{8,6},{10,8},{12,10},{14,12},{16,14},{18,... | collective-permute-start | bytes 589832 | tf_op jit(solution)/shard_map/ppermute | solution.py:12
  43.1 0.5 collective-permute-start.7
  43.6 0.9 constant_dynamic-update-slice_fusion.9
  44.5 2.3 %collective-permute-done.4 = bf16[4,192,128]{2,1,0:T(8,128)(2,1)S(1)} collective-permute-done((bf16[4,192,128]{2,1,0:T(8,128)(2,1)S(1)}, bf16[4,192,128]{2,1,0:T(8,128)(2,1)S(1)}, u32[]{:S(2)}, u32[]{:S(2)}) %collective-permute-start.4) | collective-permute-done | bytes 196640 | tf_op jit(solution)/shard_map/ppermute | solution.py:12
  46.8 0.7 constant_dynamic-update-slice_fusion.8
  47.5 1.9 %collective-permute-done.5 = bf16[4,192,128]{2,1,0:T(8,128)(2,1)S(1)} collective-permute-done((bf16[4,192,128]{2,1,0:T(8,128)(2,1)S(1)}, bf16[4,192,128]{2,1,0:T(8,128)(2,1)S(1)}, u32[]{:S(2)}, u32[]{:S(2)}) %collective-permute-start.5) | collective-permute-done | bytes 196640 | tf_op jit(solution)/shard_map/ppermute | solution.py:12
  49.5 0.7 constant_dynamic-update-slice_fusion.7
  50.2 0.7 constant_dynamic-update-slice_fusion.6
  50.8 0.7 constant_dynamic-update-slice_fusion.5
  51.5 4.9 %gather_fusion.9 = bf16[96,192,128]{2,1,0:T(8,128)(2,1)} fusion(bf16[28,192,128]{2,1,0:T(8,128)(2,1)} %constant_dynamic-update-slice_fusion.5, s32[1024]{0:T(1024)S(1)} %pad_clamp_fusion), kind=kCustom, calls=%fused_computation.13.clone | custom fusion | bytes 9437568 | tf_op jit(solution)/shard_map/jit(_take)/gather | solution.py:51
  56.5 3.0 %broadcast_select_fusion.1 = bf16[96,192,128]{2,1,0:T(8,128)(2,1)S(1)} fusion(bf16[96,192,128]{2,1,0:T(8,128)(2,1)} %gather_fusion.9, pred[96]{0:T(512)(128)(4,1)S(1)} %compare_and_fusion), kind=kLoop, calls=%fused_computation.22 | loop fusion | flops 2359296 | bytes 9437280 | tf_op jit(solution)/shard_map/jit(_take)/select_n | solution.py:51
  59.5 1.0 slice-done.3
  60.4 2.0 %fusion.18 = f32[1,1,12,192,128]{4,3,2,1,0:T(8,128)S(1)} fusion(f32[1,1,12,192,128]{4,3,2,1,0:T(8,128)S(1)} %copy-done.4, bf16[12,1536,128]{2,1,0:T(8,128)(2,1)S(1)} %bitcast.108, bf16[1,1,12,192,1536]{4,3,2,1,0:T(8,128)(2,1)S(1)} %bitcast.104), kind=kOutput, calls=%fused_computation.29 | convolution fusion | flops 906264576 | bytes 14155776 | tf_op jit(solution)/shard_map/nde,ner->ndr/dot_general | solution.py:52
  62.5 1.0 copy-done.1
  63.9 39.8 %all_gather.3 = bf16[768,128]{1,0:T(8,128)(2,1)S(1)} all-gather(bf16[24,128]{1,0:T(8,128)(2,1)S(1)} %reshape.213), channel_id=1, replica_groups=mesh['row'=16,'col'=2] {'row','col'}, dimensions={0}, use_global_device_ids=true | all-gather | bytes 202752 | tf_op jit(solution)/shard_map/all_gather | solution.py:80
  104.1 1.7 %constant_dynamic-update-slice_fusion.14 = (bf16[28,192,128]{2,1,0:T(8,128)(2,1)}, bf16[12,192,128]{2,1,0:T(8,128)(2,1)S(1)}, f32[12,192,128]{2,1,0:T(8,128)}) fusion(bf16[6,12,192]{2,1,0:T(8,128)(2,1)S(1)} %reshape_squeeze.9, bf16[12,6,128]{2,0,1:T(8,128)(2,1)S(1)} %fusion.35), kind=kOutput, calls=%fused_computation.82 | convolution fusion | flops 3833855 | bytes 2405376 | tf_op jit(solution)/shard_map/knd,nkr->ndr/dot_general | solution.py:93
  105.8 0.6 gather_fusion.13
  106.4 0.6 gather_fusion.12
  107.0 0.6 gather_fusion.11
  107.6 0.6 gather_fusion.10
  108.5 2.0 %collective-permute-start.8 = (bf16[4,192,128]{2,1,0:T(8,128)(2,1)S(1)}, bf16[4,192,128]{2,1,0:T(8,128)(2,1)S(1)}, u32[]{:S(2)}, u32[]{:S(2)}) collective-permute-start(bf16[4,192,128]{2,1,0:T(8,128)(2,1)S(1)} %broadcast_select_fusion.12), channel_id=1, source_target_pairs={{0,2},{2,4},{4,6},{6,8},{8,10},{10,12},{12,14},{14,16},{16,18},{18... | collective-permute-start | bytes 589832 | tf_op jit(solution)/shard_map/ppermute | solution.py:12
  110.7 0.5 collective-permute-start.11
  111.2 8.3 %collective-permute-done.8 = bf16[4,192,128]{2,1,0:T(8,128)(2,1)S(1)} collective-permute-done((bf16[4,192,128]{2,1,0:T(8,128)(2,1)S(1)}, bf16[4,192,128]{2,1,0:T(8,128)(2,1)S(1)}, u32[]{:S(2)}, u32[]{:S(2)}) %collective-permute-start.8) | collective-permute-done | bytes 196640 | tf_op jit(solution)/shard_map/ppermute | solution.py:12
  119.5 0.7 constant_dynamic-update-slice_fusion.13
  120.2 0.7 constant_dynamic-update-slice_fusion.12
  120.9 0.7 constant_dynamic-update-slice_fusion.11
  121.6 0.7 constant_dynamic-update-slice_fusion.10
  122.3 4.9 %gather_fusion.14 = bf16[96,192,128]{2,1,0:T(8,128)(2,1)} fusion(bf16[28,192,128]{2,1,0:T(8,128)(2,1)} %constant_dynamic-update-slice_fusion.10, s32[1024]{0:T(1024)S(1)} %pad_clamp_fusion), kind=kCustom, calls=%fused_computation.14.clone | custom fusion | bytes 9437568 | tf_op jit(solution)/shard_map/jit(_take)/gather | solution.py:51
  127.2 3.0 %broadcast_select_fusion = bf16[96,192,128]{2,1,0:T(8,128)(2,1)S(1)} fusion(bf16[96,192,128]{2,1,0:T(8,128)(2,1)} %gather_fusion.14, pred[96]{0:T(512)(128)(4,1)S(1)} %compare_and_fusion), kind=kLoop, calls=%fused_computation.21 | loop fusion | flops 2359296 | bytes 9437280 | tf_op jit(solution)/shard_map/jit(_take)/select_n | solution.py:51
  130.2 0.6 slice-done.5
  130.8 0.3 copy-done.2
  131.2 2.0 %fusion.21 = f32[1,1,12,192,128]{4,3,2,1,0:T(8,128)S(1)} fusion(f32[1,1,12,192,128]{4,3,2,1,0:T(8,128)S(1)} %copy-done.2, bf16[12,1536,128]{2,1,0:T(8,128)(2,1)S(1)} %bitcast.107, bf16[1,1,12,192,1536]{4,3,2,1,0:T(8,128)(2,1)S(1)} %bitcast.106), kind=kOutput, calls=%fused_computation.30 | convolution fusion | flops 906264576 | bytes 14155776 | tf_op jit(solution)/shard_map/nde,ner->ndr/dot_general | solution.py:52
  133.2 1.2 multiply_add_fusion.2
  134.6 1.1 copy-done.6
  135.7 0.4 copy-done.7
  136.0 1.2 add_bitcast_fusion
  (82 shorter events, 3.1 us)
Async XLA Ops:
  0.0 103.7 %copy-start = (bf16[48,768]{1,0:T(8,128)(2,1)S(1)}, bf16[48,768]{1,0:T(8,128)(2,1)}, u32[]{:S(2)}) copy-start(bf16[48,768]{1,0:T(8,128)(2,1)} %param.19) | copy-start | bytes 221188
  4.6 4.5 %copy-start.8 = (f32[1,1,12,1,64,128]{5,4,3,2,1,0:T(8,128)}, f32[1,1,12,1,64,128]{5,4,3,2,1,0:T(8,128)S(1)}, u32[]{:S(2)}) copy-start(f32[1,1,12,1,64,128]{5,4,3,2,1,0:T(8,128)S(1)} %get-tuple-element.26) | copy-start | bytes 1179652
  4.6 4.5 %copy-start.10 = (f32[1,1,12,1,64,128]{5,4,3,2,1,0:T(8,128)}, f32[1,1,12,1,64,128]{5,4,3,2,1,0:T(8,128)S(1)}, u32[]{:S(2)}) copy-start(f32[1,1,12,1,64,128]{5,4,3,2,1,0:T(8,128)S(1)} %get-tuple-element.27) | copy-start | bytes 1179652
  5.4 9.9 %copy-start.13 = (s32[1,1,12,8]{2,3,1,0:T(8,128)S(1)}, s32[1,1,12,8]{2,3,1,0:T(8,128)}, u32[]{:S(2)}) copy-start(s32[1,1,12,8]{2,3,1,0:T(8,128)} %param.15) | copy-start | bytes 1156
  5.4 10.1 %copy-start.12 = (bf16[1,1,6,2304]{3,2,1,0:T(8,128)(2,1)S(1)}, bf16[1,1,6,2304]{3,2,1,0:T(8,128)(2,1)}, u32[]{:S(2)}) copy-start(bf16[1,1,6,2304]{3,2,1,0:T(8,128)(2,1)} %param.18) | copy-start | bytes 82948
  5.5 12.0 %collective-permute-start = (bf16[4,192,128]{2,1,0:T(8,128)(2,1)S(1)}, bf16[4,192,128]{2,1,0:T(8,128)(2,1)S(1)}, u32[]{:S(2)}, u32[]{:S(2)}) collective-permute-start(bf16[4,192,128]{2,1,0:T(8,128)(2,1)S(1)} %broadcast_select_fusion.14), channel_id=1, source_target_pairs={{0,2},{2,4},{4,6},{6,8},{8,10},{10,12},{12,14},{14,16},{16,18},{18... | collective-permute-start | bytes 589832 | tf_op jit(solution)/shard_map/ppermute | solution.py:12
  9.2 9.6 %collective-permute-start.1 = (bf16[4,192,128]{2,1,0:T(8,128)(2,1)S(1)}, bf16[4,192,128]{2,1,0:T(8,128)(2,1)S(1)}, u32[]{:S(2)}, u32[]{:S(2)}) collective-permute-start(bf16[4,192,128]{2,1,0:T(8,128)(2,1)S(1)} %broadcast_select_fusion.11), channel_id=1, source_target_pairs={{0,30},{2,0},{4,2},{6,4},{8,6},{10,8},{12,10},{14,12},{16,14},{18,... | collective-permute-start | bytes 589832 | tf_op jit(solution)/shard_map/ppermute | solution.py:12
  13.9 5.5 %collective-permute-start.2 = (bf16[4,192,128]{2,1,0:T(8,128)(2,1)S(1)}, bf16[4,192,128]{2,1,0:T(8,128)(2,1)S(1)}, u32[]{:S(2)}, u32[]{:S(2)}) collective-permute-start(bf16[4,192,128]{2,1,0:T(8,128)(2,1)S(1)} %broadcast_select_fusion.8), channel_id=1, source_target_pairs={{0,1},{1,0},{2,3},{3,2},{4,5},{5,4},{6,7},{7,6},{8,9},{9,8},{10,11... | collective-permute-start | bytes 589832 | tf_op jit(solution)/shard_map/ppermute | solution.py:12
  14.7 5.4 %collective-permute-start.3 = (bf16[4,192,128]{2,1,0:T(8,128)(2,1)S(1)}, bf16[4,192,128]{2,1,0:T(8,128)(2,1)S(1)}, u32[]{:S(2)}, u32[]{:S(2)}) collective-permute-start(bf16[4,192,128]{2,1,0:T(8,128)(2,1)S(1)} %broadcast_select_fusion.5), channel_id=1, source_target_pairs={{0,1},{1,0},{2,3},{3,2},{4,5},{5,4},{6,7},{7,6},{8,9},{9,8},{10,11... | collective-permute-start | bytes 589832 | tf_op jit(solution)/shard_map/ppermute | solution.py:12
  20.9 7.9 %slice-start = ((s8[7077888]{0:T(1024)(128)(4,1)}), s8[2883584]{0:T(1024)(128)(4,1)S(1)}, s32[]{:S(2)}) async-start(s8[7077888]{0:T(1024)(128)(4,1)} %bitcast.101), calls=%async_computation | async-start | bytes 5767168
  25.8 4.0 %slice-start.1 = ((s8[7077888]{0:T(1024)(128)(4,1)}), s8[4194304]{0:T(1024)(128)(4,1)S(1)}, s32[]{:S(2)}) async-start(s8[7077888]{0:T(1024)(128)(4,1)} %bitcast.101), calls=%async_computation.1 | async-start | bytes 8388608
  25.8 4.0 %copy-start.5 = (f32[1,1,12,192,128]{4,3,2,1,0:T(8,128)S(1)}, f32[1,1,12,192,128]{4,3,2,1,0:T(8,128)}, u32[]{:S(2)}) copy-start(f32[1,1,12,192,128]{4,3,2,1,0:T(8,128)} %param.12) | copy-start | bytes 3538948
  31.8 2.9 %copy-start.3 = (f32[1,1,12,192,128]{4,3,2,1,0:T(8,128)}, f32[1,1,12,192,128]{4,3,2,1,0:T(8,128)S(1)}, u32[]{:S(2)}) copy-start(f32[1,1,12,192,128]{4,3,2,1,0:T(8,128)S(1)} %fusion.15) | copy-start | bytes 3538948
  31.8 1.3 copy-start.9
  31.8 1.5 %copy-start.11 = (f32[1,1,12,1,64,128]{5,4,3,2,1,0:T(8,128)S(1)}, f32[1,1,12,1,64,128]{5,4,3,2,1,0:T(8,128)}, u32[]{:S(2)}) copy-start(f32[1,1,12,1,64,128]{5,4,3,2,1,0:T(8,128)} %copy-done.10) | copy-start | bytes 1179652
  37.3 9.5 %collective-permute-start.4 = (bf16[4,192,128]{2,1,0:T(8,128)(2,1)S(1)}, bf16[4,192,128]{2,1,0:T(8,128)(2,1)S(1)}, u32[]{:S(2)}, u32[]{:S(2)}) collective-permute-start(bf16[4,192,128]{2,1,0:T(8,128)(2,1)S(1)} %broadcast_select_fusion.13), channel_id=1, source_target_pairs={{0,2},{2,4},{4,6},{6,8},{8,10},{10,12},{12,14},{14,16},{16,18},{18... | collective-permute-start | bytes 589832 | tf_op jit(solution)/shard_map/ppermute | solution.py:12
  38.9 10.6 %collective-permute-start.5 = (bf16[4,192,128]{2,1,0:T(8,128)(2,1)S(1)}, bf16[4,192,128]{2,1,0:T(8,128)(2,1)S(1)}, u32[]{:S(2)}, u32[]{:S(2)}) collective-permute-start(bf16[4,192,128]{2,1,0:T(8,128)(2,1)S(1)} %broadcast_select_fusion.10), channel_id=1, source_target_pairs={{0,30},{2,0},{4,2},{6,4},{8,6},{10,8},{12,10},{14,12},{16,14},{18,... | collective-permute-start | bytes 589832 | tf_op jit(solution)/shard_map/ppermute | solution.py:12
  43.1 7.1 %collective-permute-start.6 = (bf16[4,192,128]{2,1,0:T(8,128)(2,1)S(1)}, bf16[4,192,128]{2,1,0:T(8,128)(2,1)S(1)}, u32[]{:S(2)}, u32[]{:S(2)}) collective-permute-start(bf16[4,192,128]{2,1,0:T(8,128)(2,1)S(1)} %broadcast_select_fusion.7), channel_id=1, source_target_pairs={{0,1},{1,0},{2,3},{3,2},{4,5},{5,4},{6,7},{7,6},{8,9},{9,8},{10,11... | collective-permute-start | bytes 589832 | tf_op jit(solution)/shard_map/ppermute | solution.py:12
  43.1 7.7 %collective-permute-start.7 = (bf16[4,192,128]{2,1,0:T(8,128)(2,1)S(1)}, bf16[4,192,128]{2,1,0:T(8,128)(2,1)S(1)}, u32[]{:S(2)}, u32[]{:S(2)}) collective-permute-start(bf16[4,192,128]{2,1,0:T(8,128)(2,1)S(1)} %broadcast_select_fusion.4), channel_id=1, source_target_pairs={{0,1},{1,0},{2,3},{3,2},{4,5},{5,4},{6,7},{7,6},{8,9},{9,8},{10,11... | collective-permute-start | bytes 589832 | tf_op jit(solution)/shard_map/ppermute | solution.py:12
  51.5 7.9 %slice-start.2 = ((s8[7077888]{0:T(1024)(128)(4,1)}), s8[2883584]{0:T(1024)(128)(4,1)S(1)}, s32[]{:S(2)}) async-start(s8[7077888]{0:T(1024)(128)(4,1)} %bitcast.103), calls=%async_computation.2 | async-start | bytes 5767168
  56.5 4.0 %slice-start.3 = ((s8[7077888]{0:T(1024)(128)(4,1)}), s8[4194304]{0:T(1024)(128)(4,1)S(1)}, s32[]{:S(2)}) async-start(s8[7077888]{0:T(1024)(128)(4,1)} %bitcast.103), calls=%async_computation.3 | async-start | bytes 8388608
  56.5 4.0 %copy-start.4 = (f32[1,1,12,192,128]{4,3,2,1,0:T(8,128)S(1)}, f32[1,1,12,192,128]{4,3,2,1,0:T(8,128)}, u32[]{:S(2)}) copy-start(f32[1,1,12,192,128]{4,3,2,1,0:T(8,128)} %copy-done.3) | copy-start | bytes 3538948
  60.4 3.3 %copy-start.14 = (s32[1,1,12]{2,1,0:T(1,128)S(1)}, s32[1,1,12]{2,1,0:T(1,128)}, u32[]{:S(2)}) copy-start(s32[1,1,12]{2,1,0:T(1,128)} %param.17) | copy-start | bytes 148
  62.5 1.0 copy-start.1
  108.5 11.8 %collective-permute-start.9 = (bf16[4,192,128]{2,1,0:T(8,128)(2,1)S(1)}, bf16[4,192,128]{2,1,0:T(8,128)(2,1)S(1)}, u32[]{:S(2)}, u32[]{:S(2)}) collective-permute-start(bf16[4,192,128]{2,1,0:T(8,128)(2,1)S(1)} %broadcast_select_fusion.9), channel_id=1, source_target_pairs={{0,30},{2,0},{4,2},{6,4},{8,6},{10,8},{12,10},{14,12},{16,14},{18,... | collective-permute-start | bytes 589832 | tf_op jit(solution)/shard_map/ppermute | solution.py:12
  108.5 11.0 %collective-permute-start.8 = (bf16[4,192,128]{2,1,0:T(8,128)(2,1)S(1)}, bf16[4,192,128]{2,1,0:T(8,128)(2,1)S(1)}, u32[]{:S(2)}, u32[]{:S(2)}) collective-permute-start(bf16[4,192,128]{2,1,0:T(8,128)(2,1)S(1)} %broadcast_select_fusion.12), channel_id=1, source_target_pairs={{0,2},{2,4},{4,6},{6,8},{8,10},{10,12},{12,14},{14,16},{16,18},{18... | collective-permute-start | bytes 589832 | tf_op jit(solution)/shard_map/ppermute | solution.py:12
  110.6 10.3 %collective-permute-start.10 = (bf16[4,192,128]{2,1,0:T(8,128)(2,1)S(1)}, bf16[4,192,128]{2,1,0:T(8,128)(2,1)S(1)}, u32[]{:S(2)}, u32[]{:S(2)}) collective-permute-start(bf16[4,192,128]{2,1,0:T(8,128)(2,1)S(1)} %broadcast_select_fusion.6), channel_id=1, source_target_pairs={{0,1},{1,0},{2,3},{3,2},{4,5},{5,4},{6,7},{7,6},{8,9},{9,8},{10,11... | collective-permute-start | bytes 589832 | tf_op jit(solution)/shard_map/ppermute | solution.py:12
  110.7 10.9 %collective-permute-start.11 = (bf16[4,192,128]{2,1,0:T(8,128)(2,1)S(1)}, bf16[4,192,128]{2,1,0:T(8,128)(2,1)S(1)}, u32[]{:S(2)}, u32[]{:S(2)}) collective-permute-start(bf16[4,192,128]{2,1,0:T(8,128)(2,1)S(1)} %broadcast_select_fusion.3), channel_id=1, source_target_pairs={{0,1},{1,0},{2,3},{3,2},{4,5},{5,4},{6,7},{7,6},{8,9},{9,8},{10,11... | collective-permute-start | bytes 589832 | tf_op jit(solution)/shard_map/ppermute | solution.py:12
  122.3 7.9 %slice-start.4 = ((s8[7077888]{0:T(1024)(128)(4,1)}), s8[2883584]{0:T(1024)(128)(4,1)S(1)}, s32[]{:S(2)}) async-start(s8[7077888]{0:T(1024)(128)(4,1)} %bitcast.105), calls=%async_computation.4 | async-start | bytes 5767168
  127.2 3.6 %slice-start.5 = ((s8[7077888]{0:T(1024)(128)(4,1)}), s8[4194304]{0:T(1024)(128)(4,1)S(1)}, s32[]{:S(2)}) async-start(s8[7077888]{0:T(1024)(128)(4,1)} %bitcast.105), calls=%async_computation.5 | async-start | bytes 8388608
  127.2 3.9 %copy-start.2 = (f32[1,1,12,192,128]{4,3,2,1,0:T(8,128)S(1)}, f32[1,1,12,192,128]{4,3,2,1,0:T(8,128)}, u32[]{:S(2)}) copy-start(f32[1,1,12,192,128]{4,3,2,1,0:T(8,128)} %copy-done.1) | copy-start | bytes 3538948
  134.4 1.3 copy-start.6
  134.4 1.6 %copy-start.7 = (f32[1,1,12,3,64,128]{5,4,3,2,1,0:T(8,128)S(1)}, f32[1,1,12,3,64,128]{5,4,3,2,1,0:T(8,128)}, u32[]{:S(2)}) copy-start(f32[1,1,12,3,64,128]{5,4,3,2,1,0:T(8,128)} %get-tuple-element.17) | copy-start | bytes 3538948
where the time goes:
time: 138 us; the launch traced here: 137 us
  blocking collectives  39.8 us (29%)
  local copies, waits for them, and re-layouts  38.8 us (28%)
  other arithmetic  18.9 us (14%)
  starting transfers between devices  16.6 us (12%)
  waiting for transfers between devices  14.1 us (10%)
  matrix products  8.53 us (6%)
    all_gather x1, blocking collectives, body(): lax.all_gather(coarse_rhs, ('row', 'col'), axis=0, tiled=True)  39.8 us
    ppermute x12, starting transfers between devices, passed_along(): return lax.ppermute(value, axis, pairs)  16.6 us
    gather x3, local copies, waits for them, and re-layouts, apply_operator(): jnp.take(source, columns.reshape(-1), axis=0)  14.8 us
    ppermute x12, waiting for transfers between devices, passed_along(): return lax.ppermute(value, axis, pairs)  14.1 us
    unnamed x54, local copies, waits for them, and re-layouts  13.9 us
    select_n x4, other arithmetic, apply_operator(): jnp.take(source, columns.reshape(-1), axis=0)  8.92 us
    dot_general x3, matrix products, apply_operator(): jnp.einsum('nde,ner->ndr', blocks[0, 0], picked, preferred_element_type=j...  6.03 us
    add x3, other arithmetic, point_smooth(): summed + factors[:, :, component, 2, :, :, None] * pieces[:, :, :, 2]  5.29 us
  transfers between devices with their start and end apart: 12, of which 5 were waited for; matrix products, arithmetic and copies ran while one was open for 8% of the time, Pallas kernels for 0%

commit v1 on v0

v1 whole, which is shorter than its diff:
```python
import functools

import jax
import jax.numpy as jnp
from jax import lax
from jax.experimental import pallas as pl
from jax.experimental.pallas import tpu as pltpu
from jax.sharding import PartitionSpec as P

damping = 0.6
f32 = jnp.float32
bf16 = jnp.bfloat16
MESH = pl.DeviceIdType.MESH
UNROLL = 3


def iota(shape, axis):
    return lax.broadcasted_iota(jnp.int32, shape, axis)


def dot(a, b):
    return jnp.dot(a, b, preferred_element_type=f32)


def dot_first(a, b):
    return lax.dot_general(a, b, (((0,), (0,)), ((), ())), preferred_element_type=f32)


def ones_where(condition):
    return jnp.where(condition, 1.0, 0.0).astype(bf16)


def kernel(
    dims,
    rhs_hbm, smoother_ref, blocks_hbm, col_ref, send_ref, agg_ref, prolong_ref, cinv_ref,
    out_hbm,
    rhs, blocks, first, res, later, factors, small, wide,
    source1, source2, source3, packed1, packed2, pmsg, pghost, cinv32, crow, cghost, cstack,
    residual_low, pexpt, gathered, grhs, quick, out, local,
    load_sem, out_sem, h1_send, h1_recv, h2_send, h2_recv, p_send, p_recv, c_send, c_recv,
    ga_send, ga_recv, gb_send, gb_recv, gc_send, gc_recv,
):
    n_row, n_col, f1, f2, nb, dof, vec, kk, cd, agg, hb = dims
    gr = dof // 3
    cu = cd * agg
    row, col = lax.axis_index("row"), lax.axis_index("col")
    at1, at2 = row // f2, row % f2

    load_rhs = pltpu.make_async_copy(rhs_hbm.at[0, 0], rhs, load_sem.at[0])
    load_rhs.start()
    parts = 4
    load_blocks = [
        pltpu.make_async_copy(
            blocks_hbm.at[0, 0, pl.ds(p * (nb // parts), nb // parts)],
            blocks.at[pl.ds(p * (nb // parts), nb // parts)],
            load_sem.at[1 + p],
        )
        for p in range(parts)
    ]
    for load in load_blocks:
        load.start()

    row_up, row_down = (row + 1) % n_row, (row + n_row - 1) % n_row
    col_up, col_down = (col + 1) % n_col, (col + n_col - 1) % n_col
    targets = [(row_up, col), (row_down, col), (row, col_up), (row, col_down)]
    line_a = [((at1 + d) % f1 * f2 + at2, col) for d in range(1, f1)]
    line_b = [(at1 * f2 + (at2 + d) % f2, col) for d in range(1, f2)]
    line_c = [(row, (col + d) % n_col) for d in range(1, n_col)]
    greeted = targets + line_a + line_b + line_c
    barrier = pltpu.get_barrier_semaphore()
    for other in greeted:
        pl.semaphore_signal(barrier, inc=1, device_id=other, device_id_type=MESH)

    small[...] = jnp.zeros_like(small)
    for i in range(3):
        small[i * 3 : i * 3 + 3, :] = smoother_ref[0, 0, i].astype(f32)
    lanes = iota((16, 9 * vec), 1)
    starts = iota((16, 9 * vec), 0) * vec
    spread = dot_first(
        small[...].astype(bf16), ones_where((lanes >= starts) & (lanes < starts + vec))
    )
    for q in range(9):
        for n in range(nb):
            factors[q, n] = damping * spread[n * gr : (n + 1) * gr, q * vec : (q + 1) * vec]

    def smooth(n, value):
        v = [value[j * gr : (j + 1) * gr] for j in range(3)]
        return jnp.concatenate(
            [
                factors[3 * i, n] * v[0]
                + factors[3 * i + 1, n] * v[1]
                + factors[3 * i + 2, n] * v[2]
                for i in range(3)
            ],
            axis=0,
        )

    def loop(low, high, body):
        def several(step, carry):
            for u in range(UNROLL):
                body(low + step * UNROLL + u)
            return carry

        lax.fori_loop(0, (high - low) // UNROLL, several, 0)

    def multiply(n, source):
        picked = jnp.concatenate([source[col_ref[0, 0, n, k]] for k in range(kk)], axis=0)
        return dot(blocks[n], picked)

    def halo(packed, source, send_sem, recv_sem):
        return [
            pltpu.make_async_remote_copy(
                src_ref=packed.at[g],
                dst_ref=source.at[pl.ds(nb + g * hb, hb)],
                send_sem=send_sem.at[g],
                recv_sem=recv_sem.at[g],
                device_id=targets[g],
                device_id_type=MESH,
            )
            for g in range(4)
        ]

    def pack(packed):
        for g in range(4):
            for j in range(hb):
                packed[g, j] = local[send_ref[0, 0, g, j]]

    load_rhs.wait()

    def first_body(n):
        value = smooth(n, rhs[n])
        first[n] = value
        source1[n] = value.astype(bf16)
        local[n] = value.astype(bf16)

    loop(0, nb, first_body)
    pack(packed1)
    pl.semaphore_wait(barrier, len(greeted))
    halo1 = halo(packed1, source1, h1_send, h1_recv)
    for copy in halo1:
        copy.start()

    wide[...] = jnp.zeros_like(wide)
    wide[0:cd, :] = prolong_ref[0, 0].astype(f32)
    rows, modes = iota((32, 8), 0), iota((32, 8), 1)
    hit = rows < 0
    for a in range(agg):
        hit = hit | ((rows == modes + a * cd) & (modes < cd))
    lane = iota((1, nb * dof), 1)
    owner = jnp.zeros((1, nb * dof), jnp.int32)
    for n in range(nb):
        owner = jnp.where(
            (lane >= n * dof) & (lane < (n + 1) * dof), agg_ref[0, 0, n] * cd, owner
        )
    owner = jnp.broadcast_to(owner, (32, nb * dof))
    unknown = iota((32, nb * dof), 0)
    expanded = dot(ones_where(hit), wide[...].astype(bf16))
    pexpt[...] = jnp.where(
        (unknown >= owner) & (unknown < owner + cd), expanded, 0.0
    ).astype(bf16)
    upright = dot_first(pexpt[...], ones_where(iota((32, vec), 0) == iota((32, vec), 1)))
    for n in range(nb):
        source3[n] = upright[n * dof : (n + 1) * dof].astype(bf16)
    origin, place = iota((vec, vec), 0), iota((vec, vec), 1)
    for g in range(4):
        total = jnp.zeros((dof, vec), f32)
        for j in range(hb):
            shift = ones_where((place == origin + j * cu) & (origin < cu))
            total = total + dot(source3[send_ref[0, 0, g, j]], shift)
        pmsg[g] = total.astype(bf16)

    cinv32[...] = cinv_ref[...].astype(f32)

    def coarse_rows(c):
        return cinv32[pl.ds(pl.multiple_of(c * cu, 8), cu), :]

    cstack[...] = jnp.zeros_like(cstack)
    cstack[0:cu] = coarse_rows(col)
    cstack[3 * cu : 4 * cu] = coarse_rows(col_down)
    cstack[4 * cu : 5 * cu] = coarse_rows(col_up)
    crow[...] = cstack[0:32].astype(bf16)

    for copy in halo1:
        copy.wait_recv()
    crow_copies = [
        pltpu.make_async_remote_copy(
            src_ref=crow,
            dst_ref=cghost.at[g],
            send_sem=c_send.at[g],
            recv_sem=c_recv.at[g],
            device_id=targets[g],
            device_id_type=MESH,
        )
        for g in range(2)
    ]
    for copy in crow_copies:
        copy.start()
    for load in load_blocks:
        load.wait()

    def second_body(n):
        value = rhs[n] - multiply(n, source1)
        res[n] = value
        update = smooth(n, value)
        later[n] = first[n] + update
        source2[n] = update.astype(bf16)
        local[n] = update.astype(bf16)

    loop(0, nb, second_body)
    pack(packed2)
    halo2 = halo(packed2, source2, h2_send, h2_recv)
    for copy in halo2:
        copy.start()

    for copy in crow_copies:
        copy.wait_recv()
    cstack[cu : 2 * cu] = cghost[0].astype(f32)[0:cu]
    cstack[2 * cu : 3 * cu] = cghost[1].astype(f32)[0:cu]

    for copy in halo2:
        copy.wait_recv()
    pmsg_copies = [
        pltpu.make_async_remote_copy(
            src_ref=pmsg.at[g],
            dst_ref=pghost.at[g],
            send_sem=p_send.at[g],
            recv_sem=p_recv.at[g],
            device_id=targets[g],
            device_id_type=MESH,
        )
        for g in range(4)
    ]
    for copy in pmsg_copies:
        copy.start()

    def third_body(n):
        value = res[n] - multiply(n, source2)
        res[n] = value
        residual_low[pl.ds(pl.multiple_of(n * dof, dof), dof), :] = value.astype(bf16)

    loop(0, nb, third_body)
    gathered[at1, at2, col] = dot(pexpt[...], residual_low[...]).astype(bf16)

    def step_copies(line, pick, mine, others, send_sem, recv_sem):
        sends, arrivals = [], []
        for d, target in enumerate(line):
            sends.append(
                pltpu.make_async_remote_copy(
                    src_ref=pick(mine),
                    dst_ref=pick(mine),
                    send_sem=send_sem.at[d],
                    recv_sem=recv_sem.at[d],
                    device_id=target,
                    device_id_type=MESH,
                )
            )
            arrivals.append(
                pltpu.make_async_remote_copy(
                    src_ref=pick(mine),
                    dst_ref=pick(others[d]),
                    send_sem=send_sem.at[d],
                    recv_sem=recv_sem.at[d],
                    device_id=target,
                    device_id_type=MESH,
                )
            )
        return sends, arrivals

    def behind(at, count):
        return [(at + count - d) % count for d in range(1, count)]

    a_sends, a_arrivals = step_copies(
        line_a, lambda i: gathered.at[i, at2, col], at1, behind(at1, f1), ga_send, ga_recv
    )
    b_sends, b_arrivals = step_copies(
        line_b, lambda i: gathered.at[:, i, col], at2, behind(at2, f2), gb_send, gb_recv
    )
    c_sends, c_arrivals = step_copies(
        line_c, lambda i: gathered.at[:, :, i], col, behind(col, n_col), gc_send, gc_recv
    )
    for copy in a_sends:
        copy.start()

    for copy in pmsg_copies:
        copy.wait_recv()
    for g in range(4):
        for j in range(hb):
            shift = ones_where(
                (place - (1 + g) * cu == origin - j * cu)
                & (origin >= j * cu)
                & (origin < (j + 1) * cu)
            )
            source3[nb + g * hb + j] = dot(pghost[g], shift).astype(bf16)

    def fourth_body(n):
        later[n] = later[n] + smooth(n, res[n])
        value = source3[n].astype(f32) - smooth(n, multiply(n, source3))
        high = value.astype(bf16)
        quick[n, :, 0:vec] = high
        quick[n, :, vec : 2 * vec] = (value - high.astype(f32)).astype(bf16)

    third = nb // 3 // UNROLL * UNROLL
    loop(0, third, fourth_body)
    for copy in a_arrivals:
        copy.wait_recv()
    for copy in b_sends:
        copy.start()
    loop(third, 2 * third, fourth_body)
    for copy in b_arrivals:
        copy.wait_recv()
    for copy in c_sends:
        copy.start()
    loop(2 * third, nb, fourth_body)
    for copy in c_arrivals:
        copy.wait_recv()

    def unpad(step, carry):
        for c in range(n_col):
            start = pl.multiple_of((step * n_col + c) * cu, 8)
            grhs[pl.ds(start, cu), :] = gathered[step // f2, step % f2, c].astype(f32)[0:cu]
        return carry

    lax.fori_loop(0, n_row, unpad, 0)
    coarse = dot(cstack[...].astype(bf16), grhs[...].astype(bf16)).astype(bf16)
    twice = jnp.concatenate([coarse, coarse], axis=0)
    out_copies = []
    for n in range(nb):
        out[n] = later[n] + dot(quick[n], twice)
        copy = pltpu.make_async_copy(out.at[n], out_hbm.at[0, 0, n], out_sem.at[n])
        copy.start()
        out_copies.append(copy)
    for copy in halo1 + crow_copies + halo2 + pmsg_copies + a_sends + b_sends + c_sends:
        copy.wait_send()
    for copy in out_copies:
        copy.wait()


def body(rhs, smoother, blocks, col_index, send_list, agg_id, prolong, coarse_inverse):
    n_row, n_col = lax.axis_size("row"), lax.axis_size("col")
    nb, dof, vec = rhs.shape[2:]
    kk = col_index.shape[3]
    hb = send_list.shape[3]
    cd = prolong.shape[2]
    nc = coarse_inverse.shape[1]
    agg = nc // (n_row * n_col) // cd
    cu = agg * cd
    f2 = 4 if n_row % 4 == 0 else 1
    f1 = n_row // f2
    dims = (n_row, n_col, f1, f2, nb, dof, vec, kk, cd, agg, hb)
    slots = nb + 4 * hb
    field = (nb, dof, vec)
    dma = pltpu.SemaphoreType.DMA
    vmem, smem, anywhere = (
        pl.BlockSpec(memory_space=pltpu.VMEM),
        pl.BlockSpec(memory_space=pltpu.SMEM),
        pl.BlockSpec(memory_space=pl.ANY),
    )
    return pl.pallas_call(
        functools.partial(kernel, dims),
        out_shape=jax.ShapeDtypeStruct(rhs.shape, f32),
        in_specs=[anywhere, vmem, anywhere, smem, smem, smem, vmem, vmem],
        out_specs=anywhere,
        scratch_shapes=[
            pltpu.VMEM(field, f32),
            pltpu.VMEM(blocks.shape[2:], bf16),
            pltpu.VMEM(field, f32),
            pltpu.VMEM(field, f32),
            pltpu.VMEM(field, f32),
            pltpu.VMEM((9, nb, dof // 3, vec), f32),
            pltpu.VMEM((16, nb * dof // 3), f32),
            pltpu.VMEM((8, nb * dof), f32),
            pltpu.VMEM((slots, dof, vec), bf16),
            pltpu.VMEM((slots, dof, vec), bf16),
            pltpu.VMEM((slots, dof, vec), bf16),
            pltpu.VMEM((4, hb, dof, vec), bf16),
            pltpu.VMEM((4, hb, dof, vec), bf16),
            pltpu.VMEM((4, dof, vec), bf16),
            pltpu.VMEM((4, dof, vec), bf16),
            pltpu.VMEM((n_col * cu, nc), f32),
            pltpu.VMEM((32, nc), bf16),
            pltpu.VMEM((2, 32, nc), bf16),
            pltpu.VMEM((vec, nc), f32),
            pltpu.VMEM((nb * dof, vec), bf16),
            pltpu.VMEM((32, nb * dof), bf16),
            pltpu.VMEM((f1, f2, n_col, 32, vec), bf16),
            pltpu.VMEM((nc, vec), f32),
            pltpu.VMEM((nb, dof, 2 * vec), bf16),
            pltpu.VMEM(field, f32),
            pltpu.VMEM(field, bf16),
            dma((5,)),
            dma((nb,)),
            dma((4,)),
            dma((4,)),
            dma((4,)),
            dma((4,)),
            dma((4,)),
            dma((4,)),
            dma((2,)),
            dma((2,)),
            dma((max(f1 - 1, 1),)),
            dma((max(f1 - 1, 1),)),
            dma((max(f2 - 1, 1),)),
            dma((max(f2 - 1, 1),)),
            dma((n_col - 1,)),
            dma((n_col - 1,)),
        ],
        compiler_params=pltpu.CompilerParams(
            collective_id=0, has_side_effects=True, vmem_limit_bytes=56 * 1024 * 1024
        ),
    )(rhs, smoother, blocks, col_index, send_list, agg_id, prolong, coarse_inverse)


def solution(mesh):
    placed = (
        P("row", "col", None, None, None),
        P("row", "col", None, None, None),
        P("row", "col", None, None, None),
        P("row", "col", None, None),
        P("row", "col", None, None),
        P("row", "col", None),
        P("row", "col", None, None),
        P("row", None),
    )
    return jax.shard_map(
        body,
        mesh=mesh,
        in_specs=placed,
        out_specs=P("row", "col", None, None, None),
        check_vma=False,
    )
```

time: 138 us -> 53 us (0.38)
  Pallas kernels: 0 us -> 49.1 us
  blocking collectives: 39.8 us -> 0 us
  local copies, waits for them, and re-layouts: 38.8 us -> 3.72 us
  other arithmetic: 18.9 us -> 0 us
  starting transfers between devices: 16.6 us -> 0 us
  waiting for transfers between devices: 14.1 us -> 0 us
  matrix products: 8.53 us -> 0 us
    pallas_call x0 -> x1, Pallas kernels: none -> 49.1 us  [body(): pl.pallas_call(functools.partial(kernel, dims), out_shape=jax.ShapeDtypeS...]
    all_gather x1 -> x0, blocking collectives: 39.8 us -> none  [body(): lax.all_gather(coarse_rhs, ('row', 'col'), axis=0, tiled=True)]
    gather x15 -> x0, local copies, waits for them, and re-layouts: 21.8 us -> none  [the longest x3 14.8 us: apply_operator(): jnp.take(source, columns.reshape(-1), axis=0)]
    ppermute x12 -> x0, starting transfers between devices: 16.6 us -> none  [passed_along(): return lax.ppermute(value, axis, pairs)]
    ppermute x12 -> x0, waiting for transfers between devices: 14.1 us -> none  [passed_along(): return lax.ppermute(value, axis, pairs)]
    unnamed x54 -> x2, local copies, waits for them, and re-layouts: 13.9 us -> 3.72 us
    select_n x16 -> x0, other arithmetic: 9.98 us -> none  [the longest x4 8.92 us: apply_operator(): jnp.take(source, columns.reshape(-1), axis=0)]
    dot_general x8 -> x0, matrix products: 8.53 us -> none  [the longest x3 6.03 us: apply_operator(): jnp.einsum('nde,ner->ndr', blocks[0, 0], picked, preferred_element_type=j...]
  transfers between devices with their start and end apart: 12 -> 0, of which waited for: 5 -> 0; matrix products, arithmetic and copies ran while one was open for 8% -> 0% of each run, Pallas kernels for 0% -> 0%
where the time goes in v1:
time: 53 us; the launch traced here: 52.8 us
  Pallas kernels  49.1 us (93%)
  local copies, waits for them, and re-layouts  3.72 us (7%)
    pallas_call x1, Pallas kernels, body(): pl.pallas_call(functools.partial(kernel, dims), out_shape=jax.ShapeDtypeS...  49.1 us
    unnamed x2, local copies, waits for them, and re-layouts  3.72 us

profile of v1, /device:TPU:0, one launch (start us, length us, event | category | flops | bytes accessed | tf_op | source)
XLA Modules:
  0.0 52.8 jit_solution(2530429943011799621)
XLA Ops:
  0.0 1.4 %copy.9.col_ref = s32[1,1,12,8]{3,2,1,0:T(8,128)} copy(s32[1,1,12,8]{2,3,1,0:T(8,128)} %param.11) | data formatting | bytes 768 | tf_op args[3]
  1.4 49.1 %shard_map.82 = f32[1,1,12,192,128]{4,3,2,1,0:T(8,128)} custom-call(f32[1,1,12,192,128]{4,3,2,1,0:T(8,128)} %rhs_hbm.1, bf16[1,1,3,3,768]{4,3,2,1,0:T(4,128)(2,1)} %smoother_ref.1, bf16[1,1,12,192,1536]{4,3,2,1,0:T(8,128)(2,1)} %blocks_hbm.1, s32[1,1,12,8]{3,2,1,0:T(8,128)} %copy.9.col_ref, s32[1,1,4,4]{3,2,1,0:T(4,128)} %send_ref.1, s32[1,1,12]{2,1,0:T(1,128)} %agg_ref.1, ...), custom_call_target="tpu_custom_call" | custom-call | tf_op jit(solution)/shard_map/pallas_call | solution.py:358
  50.5 2.4 %copy.11 = f32[1,1,12,192,128]{4,3,2,1,0:T(8,128)} copy(f32[1,1,12,192,128]{4,3,2,1,0:T(8,128)} %shard_map.82) | data formatting | bytes 2359296

commit v2 on v1

--- a/solution.py
+++ b/solution.py
@@ -11,7 +11,7 @@
 f32 = jnp.float32
 bf16 = jnp.bfloat16
 MESH = pl.DeviceIdType.MESH
-UNROLL = 3
+UNROLL = 6
 
 
 def iota(shape, axis):
@@ -32,12 +32,12 @@
 
 def kernel(
     dims,
-    rhs_hbm, smoother_ref, blocks_hbm, col_ref, send_ref, agg_ref, prolong_ref, cinv_ref,
-    out_hbm,
-    rhs, blocks, first, res, later, factors, small, wide,
+    rhs_ref, smoother_ref, blocks_hbm, col_ref, send_ref, agg_ref, prolong_ref, cinv_ref,
+    out_ref,
+    blocks, first, res, later, factors, small, wide,
     source1, source2, source3, packed1, packed2, pmsg, pghost, cinv32, crow, cghost, cstack,
-    residual_low, pexpt, gathered, grhs, quick, out, local,
-    load_sem, out_sem, h1_send, h1_recv, h2_send, h2_recv, p_send, p_recv, c_send, c_recv,
+    residual_low, pexpt, gathered, grhs, quick, local,
+    load_sem, h1_send, h1_recv, h2_send, h2_recv, p_send, p_recv, c_send, c_recv,
     ga_send, ga_recv, gb_send, gb_recv, gc_send, gc_recv,
 ):
     n_row, n_col, f1, f2, nb, dof, vec, kk, cd, agg, hb = dims
@@ -46,14 +46,13 @@
     row, col = lax.axis_index("row"), lax.axis_index("col")
     at1, at2 = row // f2, row % f2
 
-    load_rhs = pltpu.make_async_copy(rhs_hbm.at[0, 0], rhs, load_sem.at[0])
-    load_rhs.start()
+    rhs = rhs_ref.at[0, 0]
     parts = 4
     load_blocks = [
         pltpu.make_async_copy(
             blocks_hbm.at[0, 0, pl.ds(p * (nb // parts), nb // parts)],
             blocks.at[pl.ds(p * (nb // parts), nb // parts)],
-            load_sem.at[1 + p],
+            load_sem.at[p],
         )
         for p in range(parts)
     ]
@@ -95,16 +94,16 @@
             axis=0,
         )
 
-    def loop(low, high, body):
+    def loop(low, high, body, unroll=UNROLL):
         def several(step, carry):
-            for u in range(UNROLL):
-                body(low + step * UNROLL + u)
+            for u in range(unroll):
+                body(low + step * unroll + u)
             return carry
 
-        lax.fori_loop(0, (high - low) // UNROLL, several, 0)
+        lax.fori_loop(0, (high - low) // unroll, several, 0)
 
     def multiply(n, source):
-        picked = jnp.concatenate([source[col_ref[0, 0, n, k]] for k in range(kk)], axis=0)
+        picked = jnp.concatenate([source[col_ref[0, 0, k, n]] for k in range(kk)], axis=0)
         return dot(blocks[n], picked)
 
     def halo(packed, source, send_sem, recv_sem):
@@ -125,20 +124,20 @@
             for j in range(hb):
                 packed[g, j] = local[send_ref[0, 0, g, j]]
 
-    load_rhs.wait()
-
     def first_body(n):
         value = smooth(n, rhs[n])
         first[n] = value
         source1[n] = value.astype(bf16)
-        local[n] = value.astype(bf16)
-
+
+    halo1 = halo(packed1, source1, h1_send, h1_recv)
+    for g in range(4):
+        for j in range(hb):
+            n = send_ref[0, 0, g, j]
+            packed1[g, j] = smooth(n, rhs[n]).astype(bf16)
+        if g == 0:
+            pl.semaphore_wait(barrier, len(greeted))
+        halo1[g].start()
     loop(0, nb, first_body)
-    pack(packed1)
-    pl.semaphore_wait(barrier, len(greeted))
-    halo1 = halo(packed1, source1, h1_send, h1_recv)
-    for copy in halo1:
-        copy.start()
 
     wide[...] = jnp.zeros_like(wide)
     wide[0:cd, :] = prolong_ref[0, 0].astype(f32)
@@ -195,30 +194,6 @@
     ]
     for copy in crow_copies:
         copy.start()
-    for load in load_blocks:
-        load.wait()
-
-    def second_body(n):
-        value = rhs[n] - multiply(n, source1)
-        res[n] = value
-        update = smooth(n, value)
-        later[n] = first[n] + update
-        source2[n] = update.astype(bf16)
-        local[n] = update.astype(bf16)
-
-    loop(0, nb, second_body)
-    pack(packed2)
-    halo2 = halo(packed2, source2, h2_send, h2_recv)
-    for copy in halo2:
-        copy.start()
-
-    for copy in crow_copies:
-        copy.wait_recv()
-    cstack[cu : 2 * cu] = cghost[0].astype(f32)[0:cu]
-    cstack[2 * cu : 3 * cu] = cghost[1].astype(f32)[0:cu]
-
-    for copy in halo2:
-        copy.wait_recv()
     pmsg_copies = [
         pltpu.make_async_remote_copy(
             src_ref=pmsg.at[g],
@@ -233,6 +208,48 @@
     for copy in pmsg_copies:
         copy.start()
 
+    for load in load_blocks:
+        load.wait()
+
+    def second_body(n):
+        value = rhs[n] - multiply(n, source1)
+        res[n] = value
+        update = smooth(n, value)
+        later[n] = first[n] + update
+        source2[n] = update.astype(bf16)
+        local[n] = update.astype(bf16)
+
+    loop(0, nb, second_body)
+    pack(packed2)
+    halo2 = halo(packed2, source2, h2_send, h2_recv)
+    for copy in halo2:
+        copy.start()
+
+    for copy in crow_copies:
+        copy.wait_recv()
+    cstack[cu : 2 * cu] = cghost[0].astype(f32)[0:cu]
+    cstack[2 * cu : 3 * cu] = cghost[1].astype(f32)[0:cu]
+
+    for copy in pmsg_copies:
+        copy.wait_recv()
+    for g in range(4):
+        for j in range(hb):
+            shift = ones_where(
+                (place - (1 + g) * cu == origin - j * cu)
+                & (origin >= j * cu)
+                & (origin < (j + 1) * cu)
+            )
+            source3[nb + g * hb + j] = dot(pghost[g], shift).astype(bf16)
+
+    def operator_body(n):
+        value = source3[n].astype(f32) - smooth(n, multiply(n, source3))
+        high = value.astype(bf16)
+        quick[n, :, 0:vec] = high
+        quick[n, :, vec : 2 * vec] = (value - high.astype(f32)).astype(bf16)
+
+    loop(0, nb, operator_body)
+    for copy in halo2:
+        copy.wait_recv()
     def third_body(n):
         value = res[n] - multiply(n, source2)
         res[n] = value
@@ -281,36 +298,21 @@
     for copy in a_sends:
         copy.start()
 
-    for copy in pmsg_copies:
-        copy.wait_recv()
-    for g in range(4):
-        for j in range(hb):
-            shift = ones_where(
-                (place - (1 + g) * cu == origin - j * cu)
-                & (origin >= j * cu)
-                & (origin < (j + 1) * cu)
-            )
-            source3[nb + g * hb + j] = dot(pghost[g], shift).astype(bf16)
-
     def fourth_body(n):
         later[n] = later[n] + smooth(n, res[n])
-        value = source3[n].astype(f32) - smooth(n, multiply(n, source3))
-        high = value.astype(bf16)
-        quick[n, :, 0:vec] = high
-        quick[n, :, vec : 2 * vec] = (value - high.astype(f32)).astype(bf16)
-
-    third = nb // 3 // UNROLL * UNROLL
-    loop(0, third, fourth_body)
+
+    third = nb // 3 // 2 * 2
+    loop(0, third, fourth_body, 2)
     for copy in a_arrivals:
         copy.wait_recv()
     for copy in b_sends:
         copy.start()
-    loop(third, 2 * third, fourth_body)
+    loop(third, 2 * third, fourth_body, 2)
     for copy in b_arrivals:
         copy.wait_recv()
     for copy in c_sends:
         copy.start()
-    loop(2 * third, nb, fourth_body)
+    loop(2 * third, nb, fourth_body, 2)
     for copy in c_arrivals:
         copy.wait_recv()
 
@@ -323,16 +325,10 @@
     lax.fori_loop(0, n_row, unpad, 0)
     coarse = dot(cstack[...].astype(bf16), grhs[...].astype(bf16)).astype(bf16)
     twice = jnp.concatenate([coarse, coarse], axis=0)
-    out_copies = []
     for n in range(nb):
-        out[n] = later[n] + dot(quick[n], twice)
-        copy = pltpu.make_async_copy(out.at[n], out_hbm.at[0, 0, n], out_sem.at[n])
-        copy.start()
-        out_copies.append(copy)
+        out_ref[0, 0, n] = later[n] + dot(quick[n], twice)
     for copy in halo1 + crow_copies + halo2 + pmsg_copies + a_sends + b_sends + c_sends:
         copy.wait_send()
-    for copy in out_copies:
-        copy.wait()
 
 
 def body(rhs, smoother, blocks, col_index, send_list, agg_id, prolong, coarse_inverse):
@@ -358,10 +354,9 @@
     return pl.pallas_call(
         functools.partial(kernel, dims),
         out_shape=jax.ShapeDtypeStruct(rhs.shape, f32),
-        in_specs=[anywhere, vmem, anywhere, smem, smem, smem, vmem, vmem],
-        out_specs=anywhere,
+        in_specs=[vmem, vmem, anywhere, smem, smem, smem, vmem, vmem],
+        out_specs=vmem,
         scratch_shapes=[
-            pltpu.VMEM(field, f32),
             pltpu.VMEM(blocks.shape[2:], bf16),
             pltpu.VMEM(field, f32),
             pltpu.VMEM(field, f32),
@@ -385,10 +380,8 @@
             pltpu.VMEM((f1, f2, n_col, 32, vec), bf16),
             pltpu.VMEM((nc, vec), f32),
             pltpu.VMEM((nb, dof, 2 * vec), bf16),
-            pltpu.VMEM(field, f32),
             pltpu.VMEM(field, bf16),
-            dma((5,)),
-            dma((nb,)),
+            dma((4,)),
             dma((4,)),
             dma((4,)),
             dma((4,)),
@@ -405,9 +398,9 @@
             dma((n_col - 1,)),
         ],
         compiler_params=pltpu.CompilerParams(
-            collective_id=0, has_side_effects=True, vmem_limit_bytes=56 * 1024 * 1024
+            collective_id=0, has_side_effects=True, vmem_limit_bytes=48 * 1024 * 1024
         ),
-    )(rhs, smoother, blocks, col_index, send_list, agg_id, prolong, coarse_inverse)
+    )(rhs, smoother, blocks, jnp.swapaxes(col_index, 2, 3), send_list, agg_id, prolong, coarse_inverse)
 
 
 def solution(mesh):

time: 53 us -> 55.8 us (1.053)
  the two profiles are of different devices: /device:TPU:0 before, /device:TPU:1 now
where the time goes in v2:
time: 55.8 us; the launch traced here: 55.5 us
  Pallas kernels  48.8 us (87%)
  local copies, waits for them, and re-layouts  6.68 us (12%)
    pallas_call x1, Pallas kernels, body(): pl.pallas_call(functools.partial(kernel, dims), out_shape=jax.ShapeDtypeS...  48.8 us
    unnamed x15, local copies, waits for them, and re-layouts  6.68 us

profile of v2, /device:TPU:1, one launch (start us, length us, event | category | flops | bytes accessed | tf_op | source)
XLA Modules:
  0.0 55.5 jit_solution(14712893053617640833)
XLA Ops:
  0.0 0.0 copy-start
  0.0 1.3 %copy-done = f32[1,1,12,192,128]{4,3,2,1,0:T(8,128)S(1)} copy-done((f32[1,1,12,192,128]{4,3,2,1,0:T(8,128)S(1)}, f32[1,1,12,192,128]{4,3,2,1,0:T(8,128)}, u32[]{:S(2)}) %copy-start) | copy-done | bytes 1179672
  1.3 0.0 copy-start.1
  1.3 0.9 %copy-done.1 = bf16[48,768]{1,0:T(8,128)(2,1)S(1)} copy-done((bf16[48,768]{1,0:T(8,128)(2,1)S(1)}, bf16[48,768]{1,0:T(8,128)(2,1)}, u32[]{:S(2)}) %copy-start.1) | copy-done | bytes 73752
  2.2 0.0 copy-start.2
  2.2 0.8 %copy-done.2 = bf16[1,1,6,2304]{3,2,1,0:T(8,128)(2,1)S(1)} copy-done((bf16[1,1,6,2304]{3,2,1,0:T(8,128)(2,1)S(1)}, bf16[1,1,6,2304]{3,2,1,0:T(8,128)(2,1)}, u32[]{:S(2)}) %copy-start.2) | copy-done | bytes 27672
  2.9 0.0 copy-start.3
  2.9 0.7 %copy-done.3 = bf16[1,1,3,3,768]{4,3,2,1,0:T(4,128)(2,1)S(1)} copy-done((bf16[1,1,3,3,768]{4,3,2,1,0:T(4,128)(2,1)S(1)}, bf16[1,1,3,3,768]{4,3,2,1,0:T(4,128)(2,1)}, u32[]{:S(2)}) %copy-start.3) | copy-done | bytes 13848
  3.6 0.0 copy-start.4
  3.6 0.7 %copy-done.4 = s32[1,1,12,8]{2,3,1,0:T(8,128)S(1)} copy-done((s32[1,1,12,8]{2,3,1,0:T(8,128)S(1)}, s32[1,1,12,8]{2,3,1,0:T(8,128)}, u32[]{:S(2)}) %copy-start.4) | copy-done | bytes 408
  4.3 0.0 copy-start.5
  4.3 0.7 %copy-done.5 = s32[1,1,4,4]{3,2,1,0:T(4,128)S(1)} copy-done((s32[1,1,4,4]{3,2,1,0:T(4,128)S(1)}, s32[1,1,4,4]{3,2,1,0:T(4,128)}, u32[]{:S(2)}) %copy-start.5) | copy-done | bytes 88
  5.0 0.0 copy-start.6
  5.0 0.7 %copy-done.6 = s32[1,1,12]{2,1,0:T(1,128)S(1)} copy-done((s32[1,1,12]{2,1,0:T(1,128)S(1)}, s32[1,1,12]{2,1,0:T(1,128)}, u32[]{:S(2)}) %copy-start.6) | copy-done | bytes 72
  5.7 48.8 %shard_map.82 = f32[1,1,12,192,128]{4,3,2,1,0:T(8,128)S(1)} custom-call(f32[1,1,12,192,128]{4,3,2,1,0:T(8,128)S(1)} %copy-done, bf16[1,1,3,3,768]{4,3,2,1,0:T(4,128)(2,1)S(1)} %copy-done.3, bf16[1,1,12,192,1536]{4,3,2,1,0:T(8,128)(2,1)} %blocks_hbm.1, s32[1,1,8,12]{3,2,1,0:T(8,128)S(1)} %bitcast.1, s32[1,1,4,4]{3,2,1,0:T(4,128)S(1)} %copy-done.5, ...), custom_call_target="tpu_custom_call" | custom-call | tf_op jit(solution)/shard_map/pallas_call | solution.py:354
  54.4 1.0 %copy.10 = f32[1,1,12,192,128]{4,3,2,1,0:T(8,128)} copy(f32[1,1,12,192,128]{4,3,2,1,0:T(8,128)S(1)} %shard_map.82) | data formatting | bytes 2359296
Async XLA Ops:
  0.0 1.3 %copy-start = (f32[1,1,12,192,128]{4,3,2,1,0:T(8,128)S(1)}, f32[1,1,12,192,128]{4,3,2,1,0:T(8,128)}, u32[]{:S(2)}) copy-start(f32[1,1,12,192,128]{4,3,2,1,0:T(8,128)} %rhs_ref.1) | copy-start | bytes 3538948
  1.3 0.9 %copy-start.1 = (bf16[48,768]{1,0:T(8,128)(2,1)S(1)}, bf16[48,768]{1,0:T(8,128)(2,1)}, u32[]{:S(2)}) copy-start(bf16[48,768]{1,0:T(8,128)(2,1)} %cinv_ref.1) | copy-start | bytes 221188
  2.2 0.8 %copy-start.2 = (bf16[1,1,6,2304]{3,2,1,0:T(8,128)(2,1)S(1)}, bf16[1,1,6,2304]{3,2,1,0:T(8,128)(2,1)}, u32[]{:S(2)}) copy-start(bf16[1,1,6,2304]{3,2,1,0:T(8,128)(2,1)} %prolong_ref.1) | copy-start | bytes 82948
  2.9 0.7 %copy-start.3 = (bf16[1,1,3,3,768]{4,3,2,1,0:T(4,128)(2,1)S(1)}, bf16[1,1,3,3,768]{4,3,2,1,0:T(4,128)(2,1)}, u32[]{:S(2)}) copy-start(bf16[1,1,3,3,768]{4,3,2,1,0:T(4,128)(2,1)} %smoother_ref.1) | copy-start | bytes 41476
  3.6 0.7 %copy-start.4 = (s32[1,1,12,8]{2,3,1,0:T(8,128)S(1)}, s32[1,1,12,8]{2,3,1,0:T(8,128)}, u32[]{:S(2)}) copy-start(s32[1,1,12,8]{2,3,1,0:T(8,128)} %param.11) | copy-start | bytes 1156
  4.3 0.7 %copy-start.5 = (s32[1,1,4,4]{3,2,1,0:T(4,128)S(1)}, s32[1,1,4,4]{3,2,1,0:T(4,128)}, u32[]{:S(2)}) copy-start(s32[1,1,4,4]{3,2,1,0:T(4,128)} %send_ref.1) | copy-start | bytes 196
  5.0 0.7 %copy-start.6 = (s32[1,1,12]{2,1,0:T(1,128)S(1)}, s32[1,1,12]{2,1,0:T(1,128)}, u32[]{:S(2)}) copy-start(s32[1,1,12]{2,1,0:T(1,128)} %agg_ref.1) | copy-start | bytes 148

commit v3 on v2

--- a/solution.py
+++ b/solution.py
@@ -32,12 +32,13 @@
 
 def kernel(
     dims,
-    rhs_ref, smoother_ref, blocks_hbm, col_ref, send_ref, agg_ref, prolong_ref, cinv_ref,
-    out_ref,
+    rhs_hbm, smoother_hbm, blocks_hbm, col_hbm, send_hbm, agg_hbm, prolong_hbm, cinv_hbm,
+    later_ref, quick_ref, twice_ref,
+    rhs_ref, smoother_ref, col_ref, send_ref, agg_ref, prolong_ref, cinv_ref,
     blocks, first, res, later, factors, small, wide,
     source1, source2, source3, packed1, packed2, pmsg, pghost, cinv32, crow, cghost, cstack,
     residual_low, pexpt, gathered, grhs, quick, local,
-    load_sem, h1_send, h1_recv, h2_send, h2_recv, p_send, p_recv, c_send, c_recv,
+    load_sem, out_sem, h1_send, h1_recv, h2_send, h2_recv, p_send, p_recv, c_send, c_recv,
     ga_send, ga_recv, gb_send, gb_recv, gc_send, gc_recv,
 ):
     n_row, n_col, f1, f2, nb, dof, vec, kk, cd, agg, hb = dims
@@ -46,6 +47,22 @@
     row, col = lax.axis_index("row"), lax.axis_index("col")
     at1, at2 = row // f2, row % f2
 
+    loads = [
+        pltpu.make_async_copy(source, target, load_sem.at[4 + at])
+        for at, (source, target) in enumerate(
+            [
+                (smoother_hbm, smoother_ref),
+                (rhs_hbm, rhs_ref),
+                (send_hbm, send_ref),
+                (col_hbm, col_ref),
+                (agg_hbm, agg_ref),
+                (prolong_hbm, prolong_ref),
+                (cinv_hbm, cinv_ref),
+            ]
+        )
+    ]
+    for load in loads:
+        load.start()
     rhs = rhs_ref.at[0, 0]
     parts = 4
     load_blocks = [
@@ -70,6 +87,7 @@
     for other in greeted:
         pl.semaphore_signal(barrier, inc=1, device_id=other, device_id_type=MESH)
 
+    loads[0].wait()
     small[...] = jnp.zeros_like(small)
     for i in range(3):
         small[i * 3 : i * 3 + 3, :] = smoother_ref[0, 0, i].astype(f32)
@@ -119,17 +137,14 @@
             for g in range(4)
         ]
 
-    def pack(packed):
-        for g in range(4):
-            for j in range(hb):
-                packed[g, j] = local[send_ref[0, 0, g, j]]
-
     def first_body(n):
         value = smooth(n, rhs[n])
         first[n] = value
         source1[n] = value.astype(bf16)
 
     halo1 = halo(packed1, source1, h1_send, h1_recv)
+    for load in loads[1:]:
+        load.wait()
     for g in range(4):
         for j in range(hb):
             n = send_ref[0, 0, g, j]
@@ -160,12 +175,20 @@
     upright = dot_first(pexpt[...], ones_where(iota((32, vec), 0) == iota((32, vec), 1)))
     for n in range(nb):
         source3[n] = upright[n * dof : (n + 1) * dof].astype(bf16)
-    origin, place = iota((vec, vec), 0), iota((vec, vec), 1)
+    modes, origin = iota((32, vec), 0), iota((32, vec), 1)
     for g in range(4):
-        total = jnp.zeros((dof, vec), f32)
+        total = jnp.zeros((32, dof), f32)
         for j in range(hb):
-            shift = ones_where((place == origin + j * cu) & (origin < cu))
-            total = total + dot(source3[send_ref[0, 0, g, j]], shift)
+            n = send_ref[0, 0, g, j]
+            hit = modes < 0
+            for a in range(agg):
+                hit = hit | (origin - a * cd == modes - j * cd)
+            hit = hit & (modes >= j * cd) & (modes < (j + 1) * cd) & (origin < cu)
+            total = total + lax.dot_general(
+                ones_where(hit), source3[n], (((1,), (1,)), ((), ())), preferred_element_type=f32
+            )
+            shift = (agg_ref[0, 0, n] * cd).astype(f32)
+            total = jnp.where(iota((32, dof), 0) == cu + j, shift, total)
         pmsg[g] = total.astype(bf16)
 
     cinv32[...] = cinv_ref[...].astype(f32)
@@ -180,6 +203,76 @@
     crow[...] = cstack[0:32].astype(bf16)
 
     for copy in halo1:
+        copy.wait_recv()
+    pmsg_copies = [
+        pltpu.make_async_remote_copy(
+            src_ref=pmsg.at[g],
+            dst_ref=pghost.at[g],
+            send_sem=p_send.at[g],
+            recv_sem=p_recv.at[g],
+            device_id=targets[g],
+            device_id_type=MESH,
+        )
+        for g in range(4)
+    ]
+    for copy in pmsg_copies:
+        copy.start()
+
+    for load in load_blocks:
+        load.wait()
+
+    def second_body(n):
+        value = rhs[n] - multiply(n, source1)
+        res[n] = value
+        update = smooth(n, value)
+        later[n] = first[n] + update
+        source2[n] = update.astype(bf16)
+        local[n] = update.astype(bf16)
+
+    halo2 = [
+        pltpu.make_async_remote_copy(
+            src_ref=packed2.at[g, j],
+            dst_ref=source2.at[nb + g * hb + j],
+            send_sem=h2_send.at[g * hb + j],
+            recv_sem=h2_recv.at[g * hb + j],
+            device_id=targets[g],
+            device_id_type=MESH,
+        )
+        for g in range(4)
+        for j in range(hb)
+    ]
+    for j in range(hb):
+        for g in range(2):
+            n = send_ref[0, 0, g, j]
+            packed2[g, j] = smooth(n, rhs[n] - multiply(n, source1)).astype(bf16)
+            halo2[g * hb + j].start()
+    loop(0, nb, second_body)
+    for g in range(2, 4):
+        for j in range(hb):
+            packed2[g, j] = local[send_ref[0, 0, g, j]]
+            halo2[g * hb + j].start()
+
+
+    for copy in pmsg_copies:
+        copy.wait_recv()
+    for g in range(4):
+        message = pghost[g]
+        wide_message = message.astype(f32)
+        for j in range(hb):
+            shift = wide_message[cu + j : cu + j + 1, 0:vec]
+            column = (origin - (1 + g) * cu - (modes - j * cd)).astype(f32)
+            hit = (column == shift) & (modes >= j * cd) & (modes < (j + 1) * cd)
+            source3[nb + g * hb + j] = dot_first(message, ones_where(hit)).astype(bf16)
+
+    def operator_body(n):
+        value = source3[n].astype(f32) - smooth(n, multiply(n, source3))
+        high = value.astype(bf16)
+        quick[n, :, 0:vec] = high
+        quick[n, :, vec : 2 * vec] = (value - high.astype(f32)).astype(bf16)
+
+    half = nb // 2
+    loop(0, half, operator_body, 3)
+    for copy in halo2:
         copy.wait_recv()
     crow_copies = [
         pltpu.make_async_remote_copy(
@@ -194,62 +287,6 @@
     ]
     for copy in crow_copies:
         copy.start()
-    pmsg_copies = [
-        pltpu.make_async_remote_copy(
-            src_ref=pmsg.at[g],
-            dst_ref=pghost.at[g],
-            send_sem=p_send.at[g],
-            recv_sem=p_recv.at[g],
-            device_id=targets[g],
-            device_id_type=MESH,
-        )
-        for g in range(4)
-    ]
-    for copy in pmsg_copies:
-        copy.start()
-
-    for load in load_blocks:
-        load.wait()
-
-    def second_body(n):
-        value = rhs[n] - multiply(n, source1)
-        res[n] = value
-        update = smooth(n, value)
-        later[n] = first[n] + update
-        source2[n] = update.astype(bf16)
-        local[n] = update.astype(bf16)
-
-    loop(0, nb, second_body)
-    pack(packed2)
-    halo2 = halo(packed2, source2, h2_send, h2_recv)
-    for copy in halo2:
-        copy.start()
-
-    for copy in crow_copies:
-        copy.wait_recv()
-    cstack[cu : 2 * cu] = cghost[0].astype(f32)[0:cu]
-    cstack[2 * cu : 3 * cu] = cghost[1].astype(f32)[0:cu]
-
-    for copy in pmsg_copies:
-        copy.wait_recv()
-    for g in range(4):
-        for j in range(hb):
-            shift = ones_where(
-                (place - (1 + g) * cu == origin - j * cu)
-                & (origin >= j * cu)
-                & (origin < (j + 1) * cu)
-            )
-            source3[nb + g * hb + j] = dot(pghost[g], shift).astype(bf16)
-
-    def operator_body(n):
-        value = source3[n].astype(f32) - smooth(n, multiply(n, source3))
-        high = value.astype(bf16)
-        quick[n, :, 0:vec] = high
-        quick[n, :, vec : 2 * vec] = (value - high.astype(f32)).astype(bf16)
-
-    loop(0, nb, operator_body)
-    for copy in halo2:
-        copy.wait_recv()
     def third_body(n):
         value = res[n] - multiply(n, source2)
         res[n] = value
@@ -301,18 +338,24 @@
     def fourth_body(n):
         later[n] = later[n] + smooth(n, res[n])
 
-    third = nb // 3 // 2 * 2
-    loop(0, third, fourth_body, 2)
     for copy in a_arrivals:
         copy.wait_recv()
     for copy in b_sends:
         copy.start()
-    loop(third, 2 * third, fourth_body, 2)
+    loop(0, nb, fourth_body, 4)
+    write_later = pltpu.make_async_copy(later, later_ref, out_sem.at[0])
+    write_later.start()
+    loop(half, nb, operator_body, 3)
+    write_quick = pltpu.make_async_copy(quick, quick_ref, out_sem.at[1])
+    write_quick.start()
     for copy in b_arrivals:
         copy.wait_recv()
     for copy in c_sends:
         copy.start()
-    loop(2 * third, nb, fourth_body, 2)
+    for copy in crow_copies:
+        copy.wait_recv()
+    cstack[cu : 2 * cu] = cghost[0].astype(f32)[0:cu]
+    cstack[2 * cu : 3 * cu] = cghost[1].astype(f32)[0:cu]
     for copy in c_arrivals:
         copy.wait_recv()
 
@@ -324,11 +367,12 @@
 
     lax.fori_loop(0, n_row, unpad, 0)
     coarse = dot(cstack[...].astype(bf16), grhs[...].astype(bf16)).astype(bf16)
-    twice = jnp.concatenate([coarse, coarse], axis=0)
-    for n in range(nb):
-        out_ref[0, 0, n] = later[n] + dot(quick[n], twice)
+    twice_ref[0:vec, :] = coarse
+    twice_ref[vec : 2 * vec, :] = coarse
     for copy in halo1 + crow_copies + halo2 + pmsg_copies + a_sends + b_sends + c_sends:
         copy.wait_send()
+    write_later.wait()
+    write_quick.wait()
 
 
 def body(rhs, smoother, blocks, col_index, send_list, agg_id, prolong, coarse_inverse):
@@ -346,17 +390,27 @@
     slots = nb + 4 * hb
     field = (nb, dof, vec)
     dma = pltpu.SemaphoreType.DMA
-    vmem, smem, anywhere = (
-        pl.BlockSpec(memory_space=pltpu.VMEM),
-        pl.BlockSpec(memory_space=pltpu.SMEM),
-        pl.BlockSpec(memory_space=pl.ANY),
-    )
-    return pl.pallas_call(
+    vmem = pl.BlockSpec(memory_space=pltpu.VMEM)
+    anywhere = pl.BlockSpec(memory_space=pl.ANY)
+    pinned = pl.BlockSpec(memory_space=pltpu.HBM)
+    columns = jnp.swapaxes(col_index, 2, 3)
+    later, quick, twice = pl.pallas_call(
         functools.partial(kernel, dims),
-        out_shape=jax.ShapeDtypeStruct(rhs.shape, f32),
-        in_specs=[vmem, vmem, anywhere, smem, smem, smem, vmem, vmem],
-        out_specs=vmem,
+        out_shape=[
+            jax.ShapeDtypeStruct(field, f32),
+            jax.ShapeDtypeStruct((nb, dof, 2 * vec), bf16),
+            jax.ShapeDtypeStruct((2 * vec, vec), bf16),
+        ],
+        in_specs=[pinned] * 8,
+        out_specs=[anywhere, anywhere, vmem],
         scratch_shapes=[
+            pltpu.VMEM(rhs.shape, f32),
+            pltpu.VMEM(smoother.shape, bf16),
+            pltpu.SMEM(columns.shape, jnp.int32),
+            pltpu.SMEM(send_list.shape, jnp.int32),
+            pltpu.SMEM(agg_id.shape, jnp.int32),
+            pltpu.VMEM(prolong.shape, bf16),
+            pltpu.VMEM(coarse_inverse.shape, bf16),
             pltpu.VMEM(blocks.shape[2:], bf16),
             pltpu.VMEM(field, f32),
             pltpu.VMEM(field, f32),
@@ -369,8 +423,8 @@
             pltpu.VMEM((slots, dof, vec), bf16),
             pltpu.VMEM((4, hb, dof, vec), bf16),
             pltpu.VMEM((4, hb, dof, vec), bf16),
-            pltpu.VMEM((4, dof, vec), bf16),
-            pltpu.VMEM((4, dof, vec), bf16),
+            pltpu.VMEM((4, 32, dof), bf16),
+            pltpu.VMEM((4, 32, dof), bf16),
             pltpu.VMEM((n_col * cu, nc), f32),
             pltpu.VMEM((32, nc), bf16),
             pltpu.VMEM((2, 32, nc), bf16),
@@ -381,11 +435,12 @@
             pltpu.VMEM((nc, vec), f32),
             pltpu.VMEM((nb, dof, 2 * vec), bf16),
             pltpu.VMEM(field, bf16),
+            dma((11,)),
+            dma((2,)),
             dma((4,)),
             dma((4,)),
-            dma((4,)),
-            dma((4,)),
-            dma((4,)),
+            dma((4 * hb,)),
+            dma((4 * hb,)),
             dma((4,)),
             dma((4,)),
             dma((2,)),
@@ -398,9 +453,10 @@
             dma((n_col - 1,)),
         ],
         compiler_params=pltpu.CompilerParams(
-            collective_id=0, has_side_effects=True, vmem_limit_bytes=48 * 1024 * 1024
+            collective_id=0, has_side_effects=True, vmem_limit_bytes=57 * 1024 * 1024
         ),
-    )(rhs, smoother, blocks, jnp.swapaxes(col_index, 2, 3), send_list, agg_id, prolong, coarse_inverse)
+    )(rhs, smoother, blocks, columns, send_list, agg_id, prolong, coarse_inverse)
+    return (later + dot(quick, twice))[None, None]
 
 
 def solution(mesh):

time: 55.8 us -> 47.4 us (0.85)
  the two profiles are of different devices: /device:TPU:1 before, /device:TPU:0 now
where the time goes in v3:
time: 47.4 us; the launch traced here: 47 us
  Pallas kernels  43.8 us (92%)
  matrix products  3.14 us (7%)
    pallas_call x1, Pallas kernels, body(): pl.pallas_call(functools.partial(kernel, dims), out_shape=[jax.ShapeDtype...  43.8 us
    dot_general x1, matrix products, dot(): return jnp.dot(a, b, preferred_element_type=f32)  3.14 us

profile of v3, /device:TPU:0, one launch (start us, length us, event | category | flops | bytes accessed | tf_op | source)
XLA Modules:
  0.0 47.0 jit_solution(11410038386222654370)
XLA Ops:
  0.0 43.8 %shard_map.82 = (f32[12,192,128]{2,1,0:T(8,128)}, bf16[12,192,256]{2,1,0:T(8,128)(2,1)}, bf16[256,128]{1,0:T(8,128)(2,1)}) custom-call(f32[1,1,12,192,128]{4,3,2,1,0:T(8,128)} %rhs_hbm.1, bf16[1,1,3,3,768]{4,3,2,1,0:T(4,128)(2,1)} %smoother_hbm.1, bf16[1,1,12,192,1536]{4,3,2,1,0:T(8,128)(2,1)} %blocks_hbm.1, s32[1,1,8,12]{3,2,1,0:T(8,128)} %bitcast.7, ...), custom_call_target="tpu_custom_call" | custom-call | tf_op jit(solution)/shard_map/pallas_call | solution.py:397
  43.8 3.1 %fusion = f32[1,1,12,192,128]{4,3,2,1,0:T(8,128)} fusion(f32[12,192,128]{2,1,0:T(8,128)} %get-tuple-element.8, bf16[12,192,256]{2,1,0:T(8,128)(2,1)} %get-tuple-element.9, bf16[256,128]{1,0:T(8,128)(2,1)} %get-tuple-element.10), kind=kOutput, calls=%fused_computation.1 | convolution fusion | flops 151289856 | bytes 3604480 | tf_op jit(solution)/shard_map/dot_general | solution.py:22

commit v4 on v3

--- a/solution.py
+++ b/solution.py
@@ -37,7 +37,7 @@
     rhs_ref, smoother_ref, col_ref, send_ref, agg_ref, prolong_ref, cinv_ref,
     blocks, first, res, later, factors, small, wide,
     source1, source2, source3, packed1, packed2, pmsg, pghost, cinv32, crow, cghost, cstack,
-    residual_low, pexpt, gathered, grhs, quick, local,
+    residual_low, pexpt, reduced, gathered, grhs, quick, local,
     load_sem, out_sem, h1_send, h1_recv, h2_send, h2_recv, p_send, p_recv, c_send, c_recv,
     ga_send, ga_recv, gb_send, gb_recv, gc_send, gc_recv,
 ):
@@ -191,19 +191,6 @@
             total = jnp.where(iota((32, dof), 0) == cu + j, shift, total)
         pmsg[g] = total.astype(bf16)
 
-    cinv32[...] = cinv_ref[...].astype(f32)
-
-    def coarse_rows(c):
-        return cinv32[pl.ds(pl.multiple_of(c * cu, 8), cu), :]
-
-    cstack[...] = jnp.zeros_like(cstack)
-    cstack[0:cu] = coarse_rows(col)
-    cstack[3 * cu : 4 * cu] = coarse_rows(col_down)
-    cstack[4 * cu : 5 * cu] = coarse_rows(col_up)
-    crow[...] = cstack[0:32].astype(bf16)
-
-    for copy in halo1:
-        copy.wait_recv()
     pmsg_copies = [
         pltpu.make_async_remote_copy(
             src_ref=pmsg.at[g],
@@ -221,11 +208,43 @@
     for load in load_blocks:
         load.wait()
 
+    def reduced_body(n):
+        value = dot_first(source3[n][:, 0:32], blocks[n])
+        high = value.astype(bf16)
+        reduced[n, 0:32, :] = high
+        reduced[n, 32:64, :] = (value - high.astype(f32)).astype(bf16)
+
+    loop(0, nb, reduced_body)
+    cinv32[...] = cinv_ref[...].astype(f32)
+
+    def coarse_rows(c):
+        return cinv32[pl.ds(pl.multiple_of(c * cu, 8), cu), :]
+
+    cstack[...] = jnp.zeros_like(cstack)
+    cstack[0:cu] = coarse_rows(col)
+    cstack[3 * cu : 4 * cu] = coarse_rows(col_down)
+    cstack[4 * cu : 5 * cu] = coarse_rows(col_up)
+    crow[...] = cstack[0:32].astype(bf16)
+
+    def operator_body(n):
+        value = source3[n].astype(f32) - smooth(n, multiply(n, source3))
+        high = value.astype(bf16)
+        quick[n, :, 0:vec] = high
+        quick[n, :, vec : 2 * vec] = (value - high.astype(f32)).astype(bf16)
+
+    half = nb // 2
+    for copy in halo1:
+        copy.wait_recv()
+
     def second_body(n):
         value = rhs[n] - multiply(n, source1)
         res[n] = value
         update = smooth(n, value)
         later[n] = first[n] + update
+        high = value.astype(bf16)
+        place = pl.ds(pl.multiple_of(n * dof, dof), dof)
+        residual_low[0, place, :] = high
+        residual_low[1, place, :] = (value - high.astype(f32)).astype(bf16)
         source2[n] = update.astype(bf16)
         local[n] = update.astype(bf16)
 
@@ -252,7 +271,7 @@
             packed2[g, j] = local[send_ref[0, 0, g, j]]
             halo2[g * hb + j].start()
 
-
+    before = dot(pexpt[...], residual_low[0]) + dot(pexpt[...], residual_low[1])
     for copy in pmsg_copies:
         copy.wait_recv()
     for g in range(4):
@@ -264,13 +283,6 @@
             hit = (column == shift) & (modes >= j * cd) & (modes < (j + 1) * cd)
             source3[nb + g * hb + j] = dot_first(message, ones_where(hit)).astype(bf16)
 
-    def operator_body(n):
-        value = source3[n].astype(f32) - smooth(n, multiply(n, source3))
-        high = value.astype(bf16)
-        quick[n, :, 0:vec] = high
-        quick[n, :, vec : 2 * vec] = (value - high.astype(f32)).astype(bf16)
-
-    half = nb // 2
     loop(0, half, operator_body, 3)
     for copy in halo2:
         copy.wait_recv()
@@ -287,13 +299,16 @@
     ]
     for copy in crow_copies:
         copy.start()
-    def third_body(n):
-        value = res[n] - multiply(n, source2)
-        res[n] = value
-        residual_low[pl.ds(pl.multiple_of(n * dof, dof), dof), :] = value.astype(bf16)
-
-    loop(0, nb, third_body)
-    gathered[at1, at2, col] = dot(pexpt[...], residual_low[...]).astype(bf16)
+
+    def take_off(step, total):
+        for u in range(UNROLL):
+            n = step * UNROLL + u
+            picked = jnp.concatenate([source2[col_ref[0, 0, k, n]] for k in range(kk)], axis=0)
+            total = total - dot(reduced[n], picked)
+        return total
+
+    taken = lax.fori_loop(0, nb // UNROLL, take_off, jnp.zeros((64, vec), f32))
+    gathered[at1, at2, col] = (before + (taken[0:32] + taken[32:64])).astype(bf16)
 
     def step_copies(line, pick, mine, others, send_sem, recv_sem):
         sends, arrivals = [], []
@@ -336,18 +351,16 @@
         copy.start()
 
     def fourth_body(n):
-        later[n] = later[n] + smooth(n, res[n])
-
-    for copy in a_arrivals:
-        copy.wait_recv()
-    for copy in b_sends:
-        copy.start()
-    loop(0, nb, fourth_body, 4)
-    write_later = pltpu.make_async_copy(later, later_ref, out_sem.at[0])
-    write_later.start()
+        later[n] = later[n] + smooth(n, res[n] - multiply(n, source2))
+
     loop(half, nb, operator_body, 3)
     write_quick = pltpu.make_async_copy(quick, quick_ref, out_sem.at[1])
     write_quick.start()
+    for copy in a_arrivals:
+        copy.wait_recv()
+    for copy in b_sends:
+        copy.start()
+    loop(0, half, fourth_body, 3)
     for copy in b_arrivals:
         copy.wait_recv()
     for copy in c_sends:
@@ -356,6 +369,9 @@
         copy.wait_recv()
     cstack[cu : 2 * cu] = cghost[0].astype(f32)[0:cu]
     cstack[2 * cu : 3 * cu] = cghost[1].astype(f32)[0:cu]
+    loop(half, nb, fourth_body, 3)
+    write_later = pltpu.make_async_copy(later, later_ref, out_sem.at[0])
+    write_later.start()
     for copy in c_arrivals:
         copy.wait_recv()
 
@@ -373,6 +389,11 @@
         copy.wait_send()
     write_later.wait()
     write_quick.wait()
+
+
+def finish(later_ref, quick_ref, twice_ref, out_ref):
+    for n in range(later_ref.shape[0]):
+        out_ref[0, 0, n] = later_ref[n] + dot(quick_ref[n], twice_ref[...])
 
 
 def body(rhs, smoother, blocks, col_index, send_list, agg_id, prolong, coarse_inverse):
@@ -429,8 +450,9 @@
             pltpu.VMEM((32, nc), bf16),
             pltpu.VMEM((2, 32, nc), bf16),
             pltpu.VMEM((vec, nc), f32),
-            pltpu.VMEM((nb * dof, vec), bf16),
+            pltpu.VMEM((2, nb * dof, vec), bf16),
             pltpu.VMEM((32, nb * dof), bf16),
+            pltpu.VMEM((nb, 64, kk * dof), bf16),
             pltpu.VMEM((f1, f2, n_col, 32, vec), bf16),
             pltpu.VMEM((nc, vec), f32),
             pltpu.VMEM((nb, dof, 2 * vec), bf16),
@@ -456,7 +478,19 @@
             collective_id=0, has_side_effects=True, vmem_limit_bytes=57 * 1024 * 1024
         ),
     )(rhs, smoother, blocks, columns, send_list, agg_id, prolong, coarse_inverse)
-    return (later + dot(quick, twice))[None, None]
+    rows = 3 if nb % 3 == 0 else 1
+    return pl.pallas_call(
+        finish,
+        grid=(nb // rows,),
+        out_shape=jax.ShapeDtypeStruct(rhs.shape, f32),
+        in_specs=[
+            pl.BlockSpec((rows, dof, vec), lambda n: (n, 0, 0)),
+            pl.BlockSpec((rows, dof, 2 * vec), lambda n: (n, 0, 0)),
+            pl.BlockSpec((2 * vec, vec), lambda n: (0, 0)),
+        ],
+        out_specs=pl.BlockSpec((1, 1, rows, dof, vec), lambda n: (0, 0, n, 0, 0)),
+        compiler_params=pltpu.CompilerParams(vmem_limit_bytes=57 * 1024 * 1024),
+    )(later, quick, twice)
 
 
 def solution(mesh):

time: 47.4 us -> 47.7 us (level)
  Pallas kernels: 43.8 us -> 47.5 us
  matrix products: 3.14 us -> 0 us
    pallas_call x0 -> x1, Pallas kernels: none -> 4.04 us  [body(): pl.pallas_call(finish, grid=(nb // rows,), out_shape=jax.ShapeDtypeStruct...]
    dot_general x1 -> x0, matrix products: 3.14 us -> none  [dot(): return jnp.dot(a, b, preferred_element_type=f32)]
where the time goes in v4:
time: 47.7 us; the launch traced here: 47.5 us
  Pallas kernels  47.5 us (100%)
    pallas_call x1, Pallas kernels, body(): pl.pallas_call(functools.partial(kernel, dims), out_shape=[jax.ShapeDtype...  43.5 us
    pallas_call x1, Pallas kernels, body(): pl.pallas_call(finish, grid=(nb // rows,), out_shape=jax.ShapeDtypeStruct...  4.04 us

profile of v4, /device:TPU:0, one launch (start us, length us, event | category | flops | bytes accessed | tf_op | source)
XLA Modules:
  0.0 47.5 jit_solution(8460255621270143711)
XLA Ops:
  0.0 43.5 %shard_map.82 = (f32[12,192,128]{2,1,0:T(8,128)}, bf16[12,192,256]{2,1,0:T(8,128)(2,1)}, bf16[256,128]{1,0:T(8,128)(2,1)}) custom-call(f32[1,1,12,192,128]{4,3,2,1,0:T(8,128)} %rhs_hbm.1, bf16[1,1,3,3,768]{4,3,2,1,0:T(4,128)(2,1)} %smoother_hbm.1, bf16[1,1,12,192,1536]{4,3,2,1,0:T(8,128)(2,1)} %blocks_hbm.1, s32[1,1,8,12]{3,2,1,0:T(8,128)} %bitcast.1, ...), custom_call_target="tpu_custom_call" | custom-call | tf_op jit(solution)/shard_map/pallas_call | solution.py:418
  43.5 4.0 %shard_map.83 = f32[1,1,12,192,128]{4,3,2,1,0:T(8,128)} custom-call(f32[12,192,128]{2,1,0:T(8,128)} %get-tuple-element.8.later_ref, bf16[12,192,256]{2,1,0:T(8,128)(2,1)} %get-tuple-element.9.quick_ref, bf16[256,128]{1,0:T(8,128)(2,1)} %get-tuple-element.10.twice_ref), custom_call_target="tpu_custom_call" | custom-call | tf_op jit(solution)/shard_map/pallas_call | solution.py:482

commit v5 on v4

--- a/solution.py
+++ b/solution.py
@@ -73,8 +73,6 @@
         )
         for p in range(parts)
     ]
-    for load in load_blocks:
-        load.start()
 
     row_up, row_down = (row + 1) % n_row, (row + n_row - 1) % n_row
     col_up, col_down = (col + 1) % n_col, (col + n_col - 1) % n_col
@@ -143,8 +141,10 @@
         source1[n] = value.astype(bf16)
 
     halo1 = halo(packed1, source1, h1_send, h1_recv)
-    for load in loads[1:]:
+    for load in loads[1:3]:
         load.wait()
+    for load in load_blocks:
+        load.start()
     for g in range(4):
         for j in range(hb):
             n = send_ref[0, 0, g, j]
@@ -154,6 +154,8 @@
         halo1[g].start()
     loop(0, nb, first_body)
 
+    for load in loads[3:]:
+        load.wait()
     wide[...] = jnp.zeros_like(wide)
     wide[0:cd, :] = prolong_ref[0, 0].astype(f32)
     rows, modes = iota((32, 8), 0), iota((32, 8), 1)
@@ -372,6 +374,7 @@
     loop(half, nb, fourth_body, 3)
     write_later = pltpu.make_async_copy(later, later_ref, out_sem.at[0])
     write_later.start()
+    cstack_low = cstack[...].astype(bf16)
     for copy in c_arrivals:
         copy.wait_recv()
 
@@ -382,18 +385,13 @@
         return carry
 
     lax.fori_loop(0, n_row, unpad, 0)
-    coarse = dot(cstack[...].astype(bf16), grhs[...].astype(bf16)).astype(bf16)
+    coarse = dot(cstack_low, grhs[...].astype(bf16)).astype(bf16)
     twice_ref[0:vec, :] = coarse
     twice_ref[vec : 2 * vec, :] = coarse
     for copy in halo1 + crow_copies + halo2 + pmsg_copies + a_sends + b_sends + c_sends:
         copy.wait_send()
     write_later.wait()
     write_quick.wait()
-
-
-def finish(later_ref, quick_ref, twice_ref, out_ref):
-    for n in range(later_ref.shape[0]):
-        out_ref[0, 0, n] = later_ref[n] + dot(quick_ref[n], twice_ref[...])
 
 
 def body(rhs, smoother, blocks, col_index, send_list, agg_id, prolong, coarse_inverse):
@@ -478,19 +476,7 @@
             collective_id=0, has_side_effects=True, vmem_limit_bytes=57 * 1024 * 1024
         ),
     )(rhs, smoother, blocks, columns, send_list, agg_id, prolong, coarse_inverse)
-    rows = 3 if nb % 3 == 0 else 1
-    return pl.pallas_call(
-        finish,
-        grid=(nb // rows,),
-        out_shape=jax.ShapeDtypeStruct(rhs.shape, f32),
-        in_specs=[
-            pl.BlockSpec((rows, dof, vec), lambda n: (n, 0, 0)),
-            pl.BlockSpec((rows, dof, 2 * vec), lambda n: (n, 0, 0)),
-            pl.BlockSpec((2 * vec, vec), lambda n: (0, 0)),
-        ],
-        out_specs=pl.BlockSpec((1, 1, rows, dof, vec), lambda n: (0, 0, n, 0, 0)),
-        compiler_params=pltpu.CompilerParams(vmem_limit_bytes=57 * 1024 * 1024),
-    )(later, quick, twice)
+    return (later + dot(quick, twice))[None, None]
 
 
 def solution(mesh):

time: 47.7 us -> 46.8 us (0.981)
  Pallas kernels: 47.5 us -> 43.5 us
  matrix products: 0 us -> 3.15 us
    pallas_call x1 -> x0, Pallas kernels: 4.04 us -> none  [body(): pl.pallas_call(finish, grid=(nb // rows,), out_shape=jax.ShapeDtypeStruct...]
    dot_general x0 -> x1, matrix products: none -> 3.15 us  [dot(): return jnp.dot(a, b, preferred_element_type=f32)]
where the time goes in v5:
time: 46.8 us; the launch traced here: 46.6 us
  Pallas kernels  43.5 us (93%)
  matrix products  3.15 us (7%)
    pallas_call x1, Pallas kernels, body(): pl.pallas_call(functools.partial(kernel, dims), out_shape=[jax.ShapeDtype...  43.5 us
    dot_general x1, matrix products, dot(): return jnp.dot(a, b, preferred_element_type=f32)  3.15 us

profile of v5, /device:TPU:0, one launch (start us, length us, event | category | flops | bytes accessed | tf_op | source)
XLA Modules:
  0.0 46.6 jit_solution(16186462992326313191)
XLA Ops:
  0.0 43.5 %shard_map.82 = (f32[12,192,128]{2,1,0:T(8,128)}, bf16[12,192,256]{2,1,0:T(8,128)(2,1)}, bf16[256,128]{1,0:T(8,128)(2,1)}) custom-call(f32[1,1,12,192,128]{4,3,2,1,0:T(8,128)} %rhs_hbm.1, bf16[1,1,3,3,768]{4,3,2,1,0:T(4,128)(2,1)} %smoother_hbm.1, bf16[1,1,12,192,1536]{4,3,2,1,0:T(8,128)(2,1)} %blocks_hbm.1, s32[1,1,8,12]{3,2,1,0:T(8,128)} %bitcast.7, ...), custom_call_target="tpu_custom_call" | custom-call | tf_op jit(solution)/shard_map/pallas_call | solution.py:416
  43.5 3.1 %fusion = f32[1,1,12,192,128]{4,3,2,1,0:T(8,128)} fusion(f32[12,192,128]{2,1,0:T(8,128)} %get-tuple-element.8, bf16[12,192,256]{2,1,0:T(8,128)(2,1)} %get-tuple-element.9, bf16[256,128]{1,0:T(8,128)(2,1)} %get-tuple-element.10), kind=kOutput, calls=%fused_computation.1 | convolution fusion | flops 151289856 | bytes 3604480 | tf_op jit(solution)/shard_map/dot_general | solution.py:22

commit v6 on v5

--- a/solution.py
+++ b/solution.py
@@ -355,14 +355,15 @@
     def fourth_body(n):
         later[n] = later[n] + smooth(n, res[n] - multiply(n, source2))
 
-    loop(half, nb, operator_body, 3)
+    loop(half, half + 3, operator_body, 3)
     write_quick = pltpu.make_async_copy(quick, quick_ref, out_sem.at[1])
-    write_quick.start()
     for copy in a_arrivals:
         copy.wait_recv()
     for copy in b_sends:
         copy.start()
-    loop(0, half, fourth_body, 3)
+    loop(half + 3, nb, operator_body, 3)
+    write_quick.start()
+    loop(0, 3, fourth_body, 3)
     for copy in b_arrivals:
         copy.wait_recv()
     for copy in c_sends:
@@ -371,7 +372,7 @@
         copy.wait_recv()
     cstack[cu : 2 * cu] = cghost[0].astype(f32)[0:cu]
     cstack[2 * cu : 3 * cu] = cghost[1].astype(f32)[0:cu]
-    loop(half, nb, fourth_body, 3)
+    loop(3, nb, fourth_body, 3)
     write_later = pltpu.make_async_copy(later, later_ref, out_sem.at[0])
     write_later.start()
     cstack_low = cstack[...].astype(bf16)

time: 46.8 us -> 47.4 us (1.013)
  Pallas kernels: 43.5 us -> 44.1 us
    pallas_call x1, Pallas kernels: 43.5 us -> 44.1 us  [body(): pl.pallas_call(functools.partial(kernel, dims), out_shape=[jax.ShapeDtype...]
where the time goes in v6:
time: 47.4 us; the launch traced here: 47.2 us
  Pallas kernels  44.1 us (93%)
  matrix products  3.15 us (7%)
    pallas_call x1, Pallas kernels, body(): pl.pallas_call(functools.partial(kernel, dims), out_shape=[jax.ShapeDtype...  44.1 us
    dot_general x1, matrix products, dot(): return jnp.dot(a, b, preferred_element_type=f32)  3.15 us

profile of v6, /device:TPU:0, one launch (start us, length us, event | category | flops | bytes accessed | tf_op | source)
XLA Modules:
  0.0 47.2 jit_solution(4025649704333845010)
XLA Ops:
  0.0 44.1 %shard_map.82 = (f32[12,192,128]{2,1,0:T(8,128)}, bf16[12,192,256]{2,1,0:T(8,128)(2,1)}, bf16[256,128]{1,0:T(8,128)(2,1)}) custom-call(f32[1,1,12,192,128]{4,3,2,1,0:T(8,128)} %rhs_hbm.1, bf16[1,1,3,3,768]{4,3,2,1,0:T(4,128)(2,1)} %smoother_hbm.1, bf16[1,1,12,192,1536]{4,3,2,1,0:T(8,128)(2,1)} %blocks_hbm.1, s32[1,1,8,12]{3,2,1,0:T(8,128)} %bitcast.7, ...), custom_call_target="tpu_custom_call" | custom-call | tf_op jit(solution)/shard_map/pallas_call | solution.py:417
  44.1 3.2 %fusion = f32[1,1,12,192,128]{4,3,2,1,0:T(8,128)} fusion(f32[12,192,128]{2,1,0:T(8,128)} %get-tuple-element.8, bf16[12,192,256]{2,1,0:T(8,128)(2,1)} %get-tuple-element.9, bf16[256,128]{1,0:T(8,128)(2,1)} %get-tuple-element.10), kind=kOutput, calls=%fused_computation.1 | convolution fusion | flops 151289856 | bytes 3604480 | tf_op jit(solution)/shard_map/dot_general | solution.py:22
